TPU v7x, 32 devices: a whole 2x2x4 slice. The times are simulated.
32 devices in a mesh: section: 2 (over x), dp: 16 (over z, y, core).
Axes of the slice: x: 2, y: 2, z: 4, core: 2. Of those that a mesh axis runs over, the one named last changes fastest.
Arguments:
- block_input: bfloat16 [2, 1024, 1024], P(None, 'dp'), may hold values from -6 to 6
- crop_ids: int32 [2, 1024], P(None, 'dp'), may hold values from -1 to 1, as said below
- out_grad: bfloat16 [2, 1024, 1024], P(None, 'dp'), may hold values from -6 to 6
- norm1_gain: bfloat16 [2, 1024], P('section', 'dp'), may hold values from 0.099609375 to 1.8984375
- norm1_shift: bfloat16 [2, 1024], P('section', 'dp'), may hold values from -3 to 3
- w_qkv: bfloat16 [2, 1024, 3072], P('section', 'dp'), may hold values from -0.1875 to 0.1875
- w_out: bfloat16 [2, 1024, 1024], P('section', 'dp'), may hold values from -0.75 to 0.75
- b_out: bfloat16 [2, 1024], P('section', 'dp'), may hold values from -3 to 3
- norm2_gain: bfloat16 [2, 1024], P('section', 'dp'), may hold values from 0.099609375 to 1.8984375
- norm2_shift: bfloat16 [2, 1024], P('section', 'dp'), may hold values from -3 to 3
- w_up: bfloat16 [2, 1024, 4096], P('section', 'dp'), may hold values from -0.1875 to 0.1875
- b_up: bfloat16 [2, 4096], P('section', 'dp'), may hold values from -3 to 3
- w_down: bfloat16 [2, 4096, 1024], P('section', 'dp'), may hold values from -0.09375 to 0.09375
- b_down: bfloat16 [2, 1024], P('section', 'dp'), may hold values from -3 to 3
Outputs:
- layer_outputs: bfloat16 [2, 2, 1024, 1024], P('section', None, 'dp')
- input_grads: bfloat16 [2, 2, 1024, 1024], P('section', None, 'dp')
- grad_norm1_gain: float32 [2, 1024], P('section', 'dp')
- grad_norm1_shift: float32 [2, 1024], P('section', 'dp')
- grad_w_qkv: float32 [2, 1024, 3072], P('section', 'dp')
- grad_w_out: float32 [2, 1024, 1024], P('section', 'dp')
- grad_b_out: float32 [2, 1024], P('section', 'dp')
- grad_norm2_gain: float32 [2, 1024], P('section', 'dp')
- grad_norm2_shift: float32 [2, 1024], P('section', 'dp')
- grad_w_up: float32 [2, 1024, 4096], P('section', 'dp')
- grad_b_up: float32 [2, 4096], P('section', 'dp')
- grad_w_down: float32 [2, 4096, 1024], P('section', 'dp')
- grad_b_down: float32 [2, 1024], P('section', 'dp')
Inputs may be any that keep to these rules, and one draw needn't show every extreme that they name: `crop_ids`: within each block of 64 rows of one micro-batch and one device, crops are numbered from 0 in row order: first one or more global crops of 50 rows (never more than fit in 64 rows), then local crops of 10 rows that fill the remaining room but for at most two crops' worth, then padding rows marked -1; blocks are independent.
All inputs are finite; a program needn't handle non-finite values.
Results may differ from a plain program's by a relative error of at most 0.015.
Values may be sent and summed in bfloat16 or wider, within the bound.
A program may use at most 256 MiB of HBM per device.

v0:
```python
import jax
import jax.numpy as jnp
from jax import lax
from jax.sharding import PartitionSpec as P

HEAD = 64


def passed_along(x, axis, by):
    devices = lax.axis_size(axis)
    pairs = [(i, i + by) for i in range(devices) if 0 <= i + by < devices]
    return lax.ppermute(x, axis, pairs)


def norm_rows(values, gain, shift):
    centred = values - jnp.mean(values, axis=-1, keepdims=True)
    spread = jnp.mean(centred * centred, axis=-1, keepdims=True)
    return centred * lax.rsqrt(spread + 1e-06) * gain + shift


def gelu_exact(values):
    return jax.nn.gelu(values, approximate=False)


def inner_rows(left, right):
    return lax.dot_general(
        left, right, (((0,), (0,)), ((), ())), preferred_element_type=jnp.float32
    )


def times_transpose(left, right):
    return lax.dot_general(
        left, right, (((1,), (1,)), ((), ())), preferred_element_type=jnp.float32
    )


def split_heads(qkv_rows):
    model_width = qkv_rows.shape[1] // 3
    head_count = model_width // HEAD
    queries = qkv_rows[:, :model_width].reshape(-1, head_count, HEAD)
    key_rows = qkv_rows[:, model_width : 2 * model_width].reshape(-1, head_count, HEAD)
    value_rows = qkv_rows[:, 2 * model_width :].reshape(-1, head_count, HEAD)
    return (queries, key_rows, value_rows)


def head_scores(qkv_rows, crop_rows):
    queries, key_rows, value_rows = split_heads(qkv_rows)
    scores = jnp.einsum("qhd,khd->hqk", queries, key_rows, preferred_element_type=jnp.float32)
    scores = scores * HEAD ** (-0.5)
    same_crop = crop_rows[:, None] == crop_rows[None, :]
    return jnp.where(same_crop[None], scores, -1e30)


def forward_layer(layer_in, crop_rows, weights):
    gain_one, shift_one, w_qkv, w_out, b_out, gain_two, shift_two, w_up, b_up, w_down, b_down = (
        weights
    )
    row_count = layer_in.shape[0]
    normed = norm_rows(
        layer_in, gain_one.astype(jnp.float32), shift_one.astype(jnp.float32)
    ).astype(jnp.bfloat16)
    qkv_rows = jnp.dot(normed, w_qkv, preferred_element_type=jnp.float32).astype(jnp.bfloat16)
    scores = head_scores(qkv_rows, crop_rows)
    row_peak = jnp.max(scores, axis=-1, keepdims=True)
    log_total = row_peak + jnp.log(jnp.sum(jnp.exp(scores - row_peak), axis=-1, keepdims=True))
    softmax_low = jnp.exp(scores - log_total).astype(jnp.bfloat16)
    queries, key_rows, value_rows = split_heads(qkv_rows)
    mixed_heads = jnp.einsum(
        "hqk,khd->qhd", softmax_low, value_rows, preferred_element_type=jnp.float32
    )
    mixed_heads = mixed_heads.reshape(row_count, -1).astype(jnp.bfloat16)
    hidden = (
        layer_in
        + jnp.dot(mixed_heads, w_out, preferred_element_type=jnp.float32)
        + b_out.astype(jnp.float32)
    )
    squeezed = norm_rows(
        hidden, gain_two.astype(jnp.float32), shift_two.astype(jnp.float32)
    ).astype(jnp.bfloat16)
    up_rows = jnp.dot(squeezed, w_up, preferred_element_type=jnp.float32) + b_up.astype(jnp.float32)
    active = gelu_exact(up_rows).astype(jnp.bfloat16)
    result = (
        hidden
        + jnp.dot(active, w_down, preferred_element_type=jnp.float32)
        + b_down.astype(jnp.float32)
    )
    return (
        layer_in,
        normed,
        qkv_rows,
        log_total,
        mixed_heads,
        hidden,
        squeezed,
        up_rows,
        active,
        result,
    )


def backward_feed(grad_result, saved, weights):
    gain_one, shift_one, w_qkv, w_out, b_out, gain_two, shift_two, w_up, b_up, w_down, b_down = (
        weights
    )
    (
        layer_in,
        normed,
        qkv_rows,
        log_total,
        mixed_heads,
        hidden,
        squeezed,
        up_rows,
        active,
        result,
    ) = saved
    grad_branch = grad_result.astype(jnp.bfloat16)
    grad_w_down = inner_rows(active, grad_branch)
    grad_b_down = jnp.sum(grad_branch.astype(jnp.float32), axis=0)
    grad_active = times_transpose(grad_branch, w_down)
    gelu_value, gelu_pull = jax.vjp(gelu_exact, up_rows)
    grad_up = gelu_pull(grad_active)[0].astype(jnp.bfloat16)
    grad_w_up = inner_rows(squeezed, grad_up)
    grad_b_up = jnp.sum(grad_up.astype(jnp.float32), axis=0)
    grad_squeezed = times_transpose(grad_up, w_up)
    norm_value, norm_pull = jax.vjp(
        norm_rows, hidden, gain_two.astype(jnp.float32), shift_two.astype(jnp.float32)
    )
    grad_hid, grad_gain_two, grad_shift_two = norm_pull(grad_squeezed)
    grad_hidden = grad_result + grad_hid
    return (
        grad_hidden,
        (grad_gain_two, grad_shift_two, grad_w_up, grad_b_up, grad_w_down, grad_b_down),
    )


def backward_attend(grad_hidden, saved, crop_rows, weights):
    gain_one, shift_one, w_qkv, w_out, b_out, gain_two, shift_two, w_up, b_up, w_down, b_down = (
        weights
    )
    (
        layer_in,
        normed,
        qkv_rows,
        log_total,
        mixed_heads,
        hidden,
        squeezed,
        up_rows,
        active,
        result,
    ) = saved
    row_count = layer_in.shape[0]
    grad_attn = grad_hidden.astype(jnp.bfloat16)
    grad_w_out = inner_rows(mixed_heads, grad_attn)
    grad_b_out = jnp.sum(grad_attn.astype(jnp.float32), axis=0)
    grad_mixed = times_transpose(grad_attn, w_out).astype(jnp.bfloat16)
    queries, key_rows, value_rows = split_heads(qkv_rows)
    grad_mixed = grad_mixed.reshape(queries.shape)
    softmax_out = jnp.exp(head_scores(qkv_rows, crop_rows) - log_total)
    grad_soft = jnp.einsum(
        "qhd,khd->hqk", grad_mixed, value_rows, preferred_element_type=jnp.float32
    )
    grad_values = jnp.einsum(
        "hqk,qhd->khd",
        softmax_out.astype(jnp.bfloat16),
        grad_mixed,
        preferred_element_type=jnp.float32,
    )
    row_centre = jnp.sum(grad_soft * softmax_out, axis=-1, keepdims=True)
    grad_scores = (softmax_out * (grad_soft - row_centre)).astype(jnp.bfloat16)
    grad_queries = jnp.einsum(
        "hqk,khd->qhd", grad_scores, key_rows, preferred_element_type=jnp.float32
    ) * HEAD ** (-0.5)
    grad_keys = jnp.einsum(
        "hqk,qhd->khd", grad_scores, queries, preferred_element_type=jnp.float32
    ) * HEAD ** (-0.5)
    grad_qkv = jnp.concatenate(
        [
            grad_queries.reshape(row_count, -1),
            grad_keys.reshape(row_count, -1),
            grad_values.reshape(row_count, -1),
        ],
        axis=1,
    ).astype(jnp.bfloat16)
    grad_w_qkv = inner_rows(normed, grad_qkv)
    grad_normed = times_transpose(grad_qkv, w_qkv)
    first_value, first_pull = jax.vjp(
        norm_rows, layer_in, gain_one.astype(jnp.float32), shift_one.astype(jnp.float32)
    )
    grad_in, grad_gain_one, grad_shift_one = first_pull(grad_normed)
    return (
        grad_hidden + grad_in,
        (grad_gain_one, grad_shift_one, grad_w_qkv, grad_w_out, grad_b_out),
    )


def local(
    block_input,
    crop_ids,
    out_grad,
    norm1_gain,
    norm1_shift,
    w_qkv,
    w_out,
    b_out,
    norm2_gain,
    norm2_shift,
    w_up,
    b_up,
    w_down,
    b_down,
):
    is_first = lax.axis_index("section") == 0
    shards = (
        norm1_gain,
        norm1_shift,
        w_qkv,
        w_out,
        b_out,
        norm2_gain,
        norm2_shift,
        w_up,
        b_up,
        w_down,
        b_down,
    )
    gathered = (
        lax.all_gather(shards[0], "dp", axis=1, tiled=True),
        lax.all_gather(shards[1], "dp", axis=1, tiled=True),
        lax.all_gather(shards[2], "dp", axis=1, tiled=True),
        lax.all_gather(shards[3], "dp", axis=1, tiled=True),
        lax.all_gather(shards[4], "dp", axis=1, tiled=True),
        lax.all_gather(shards[5], "dp", axis=1, tiled=True),
        lax.all_gather(shards[6], "dp", axis=1, tiled=True),
        lax.all_gather(shards[7], "dp", axis=1, tiled=True),
        lax.all_gather(shards[8], "dp", axis=1, tiled=True),
        lax.all_gather(shards[9], "dp", axis=1, tiled=True),
        lax.all_gather(shards[10], "dp", axis=1, tiled=True),
    )
    weights = tuple((item[0] for item in gathered))
    micro_count = block_input.shape[0]

    def pick(upper, lower):
        return jax.tree.map(
            lambda later, earlier: jnp.where(is_first, earlier, later), upper, lower
        )

    incoming = jnp.zeros(block_input.shape[1:], jnp.bfloat16)
    records = []
    kept_saved = []
    forward_rows = []
    for step_index in range(micro_count + 1):
        own_rows = block_input[min(step_index, micro_count - 1)]
        source = jnp.where(is_first, own_rows, incoming)
        crop_rows = jnp.where(
            is_first, crop_ids[min(step_index, micro_count - 1)], crop_ids[max(step_index - 1, 0)]
        )
        saved = forward_layer(source.astype(jnp.float32), crop_rows, weights)
        sent_rows = saved[-1].astype(jnp.bfloat16)
        forward_rows.append(sent_rows)
        records.append((source, crop_rows))
        kept_saved.append(saved)
        if step_index < micro_count:
            incoming = passed_along(sent_rows, "section", 1)
    layer_outputs = jnp.where(
        is_first, jnp.stack(forward_rows[:micro_count]), jnp.stack(forward_rows[1:])
    )
    totals = jax.tree.map(lambda item: jnp.zeros(item.shape, jnp.float32), weights)
    back_in = jnp.zeros(block_input.shape[1:], jnp.bfloat16)
    backward_rows = []
    for step_index in range(micro_count + 1):
        late_tick = min(step_index + 1, micro_count)
        early_tick = max(step_index - 1, 0)
        source, crop_rows = pick(records[late_tick], records[early_tick])
        saved = pick(kept_saved[late_tick], kept_saved[early_tick])
        if step_index < micro_count:
            last_grad = out_grad[step_index]
        else:
            last_grad = jnp.zeros_like(out_grad[0])
        cotangent = jnp.where(is_first, back_in, last_grad)
        grad_hidden, feed_grads = backward_feed(cotangent.astype(jnp.float32), saved, weights)
        feed_totals = tuple((left + right for left, right in zip(totals[5:], feed_grads)))
        grad_in, attend_grads = backward_attend(grad_hidden, saved, crop_rows, weights)
        attend_totals = tuple((left + right for left, right in zip(totals[:5], attend_grads)))
        totals = attend_totals + feed_totals
        sent_grad = grad_in.astype(jnp.bfloat16)
        backward_rows.append(sent_grad)
        if step_index < micro_count:
            back_in = passed_along(sent_grad, "section", -1)
    input_grads = jnp.where(
        is_first, jnp.stack(backward_rows[1:]), jnp.stack(backward_rows[:micro_count])
    )
    summed = lax.psum_scatter(totals, "dp", scatter_dimension=0, tiled=True)
    outputs = tuple((item[None] for item in summed))
    return (layer_outputs[None], input_grads[None]) + outputs


def solution(mesh):
    in_specs = (
        P(None, "dp", None),
        P(None, "dp"),
        P(None, "dp", None),
        P("section", "dp"),
        P("section", "dp"),
        P("section", "dp", None),
        P("section", "dp", None),
        P("section", "dp"),
        P("section", "dp"),
        P("section", "dp"),
        P("section", "dp", None),
        P("section", "dp"),
        P("section", "dp", None),
        P("section", "dp"),
    )
    out_specs = (
        P("section", None, "dp", None),
        P("section", None, "dp", None),
        P("section", "dp"),
        P("section", "dp"),
        P("section", "dp", None),
        P("section", "dp", None),
        P("section", "dp"),
        P("section", "dp"),
        P("section", "dp"),
        P("section", "dp", None),
        P("section", "dp"),
        P("section", "dp", None),
        P("section", "dp"),
    )
    return jax.shard_map(local, mesh=mesh, in_specs=in_specs, out_specs=out_specs, check_vma=False)
```

profile of v0, /device:TPU:0, one launch (start us, length us, event | category | flops | bytes accessed | tf_op | source)
XLA Modules:
  0.0 1024.1 jit_solution(4464706458577702938)
XLA Ops:
  17.1 64.3 %all-reduce.14 = (bf16[1024]{0:T(1024)(128)(2,1)S(1)}, bf16[1024]{0:T(1024)(128)(2,1)S(1)}, bf16[1024]{0:T(1024)(128)(2,1)S(1)}, bf16[1024]{0:T(1024)(128)(2,1)S...) all-reduce(bf16[1024]{0:T(1024)(128)(2,1)S(1)} %dynamic-update-slic, ...), channel_id=1, replica_groups=mesh['section'=2,'dp'=16] {'dp'}, use_global_device_ids=true, to_apply=%add.1 | all-reduce | flops 6144 | bytes 24576
  81.4 17.4 %all_gather.41 = bf16[1,4096]{1,0:T(2,128)(2,1)S(1)} all-gather(bf16[1,256]{1,0:T(2,128)(2,1)} %param.25), channel_id=1, replica_groups=mesh['section'=2,'dp'=16] {'dp'}, dimensions={1}, use_global_device_ids=true | all-gather | bytes 8704 | tf_op jit(solution)/shard_map/all_gather | solution.py:237
  105.7 4.2 fusion.45
  111.2 6.6 all-gather.7.cloned.1.call-done
  117.8 2.2 fusion.361
  120.2 73.4 %all-gather.9.cloned.1.call-done = bf16[1,1024,4096]{2,1,0:T(8,128)(2,1)} async-done(((bf16[1,64,4096]{2,1,0:T(8,128)(2,1)}), bf16[1,1024,4096]{2,1,0:T(8,128)(2,1)}) %all-gather.9.cloned.1.call-update) | async-done | bytes 8388624 | tf_op jit(solution)/shard_map/all_gather | solution.py:236
  193.7 5.0 fusion.36
  198.8 70.1 %all-gather.11.cloned.1.call-done = bf16[1,4096,1024]{2,1,0:T(8,128)(2,1)} async-done(((bf16[1,256,1024]{2,1,0:T(8,128)(2,1)}), bf16[1,4096,1024]{2,1,0:T(8,128)(2,1)}) %all-gather.11.cloned.1.call-update) | async-done | bytes 8388624 | tf_op jit(solution)/shard_map/all_gather | solution.py:238
  268.9 5.7 fusion.141
  274.7 3.7 collective-permute-start
  278.5 2.8 collective-permute-done
  282.2 4.8 broadcast_select_fusion.2
  297.8 5.1 fusion.39
  303.4 3.4 fusion.138
  306.9 4.9 collective-permute-start.1
  311.9 5.3 convert_reduce_fusion.2
  317.2 3.3 multiply_reduce_fusion.5
  326.2 2.1 convolution_convert_fusion.2
  330.8 2.0 fusion.89
  343.1 5.7 multiply_reduce_fusion.8
  351.0 2.3 convert_reduce_fusion.8
  355.3 3.3 broadcast_select_fusion
  365.3 2.0 broadcast_select_fusion.3
  367.3 2.2 fusion.365
  370.2 2.8 fusion.366
  374.3 5.1 fusion.42
  381.6 5.5 convert_reduce_fusion.1
  387.1 3.3 multiply_reduce_fusion.4
  410.9 5.6 multiply_reduce_fusion.7
  421.4 4.6 collective-permute-done.3
  426.0 8.6 convert_reduce_fusion
  434.6 3.3 multiply_reduce_fusion.3
  438.9 2.8 add_add_fusion.3
  447.2 8.1 fusion.278
  455.3 6.5 fusion.277
  469.3 14.7 %add_add_fusion.2 = f32[1024,3072]{1,0:T(8,128)} fusion(f32[1024,3072]{1,0:T(8,128)} %fusion.278, f32[1024,3072]{1,0:T(8,128)} %fusion.277, bf16[64,1024]{1,0:T(8,128)(2,1)S(1)} %copy.188, bf16[64,1024]{1,0:T(8,128)(2,1)S(1)} %reshape.859, bf16[64,1024]{1,0:T(8,128)(2,1)S(1)} %reshape.858, pred[]{:T(512)S(6)} %eq.107, ...), kind=kOutput, calls=%fused_computation.2 | convolution fusion | flops 410976256 | bytes 38413312 | tf_op jit(solution)/shard_map/dot_general | solution.py:26
  485.1 8.2 fusion.289
  493.2 8.2 fusion.287
  501.4 18.9 %add_add_fusion.1 = f32[1024,4096]{1,0:T(8,128)} fusion(f32[1024,4096]{1,0:T(8,128)} %fusion.289, f32[1024,4096]{1,0:T(8,128)} %fusion.287, bf16[64,4096]{1,0:T(8,128)(2,1)S(1)} %copy-done.26, bf16[64,1024]{1,0:T(8,128)(2,1)S(1)} %get-tuple-element.114, bf16[64,1024]{1,0:T(8,128)(2,1)S(1)} %copy-done.10, pred[]{:T(512)S(6)} %eq.107), kind=kOutput, calls=%fused_computation.1 | convolution fusion | flops 545325056 | bytes 51118080 | tf_op jit(solution)/shard_map/dot_general | solution.py:26
  522.4 11.5 %fusion.222 = f32[4096,1024]{1,0:T(8,128)} fusion(pred[]{:T(512)S(6)} %eq.107, bf16[2,64,1024]{2,1,0:T(8,128)(2,1)S(1)} %copy-done.66, f32[64,4096]{1,0:T(8,128)S(1)} %copy-done.57, f32[64,4096]{1,0:T(8,128)S(1)} %copy-done.54), kind=kOutput, calls=%fused_computation.245 | convolution fusion | flops 571277312 | bytes 19006464 | tf_op jit(solution)/shard_map/dot_general | solution.py:26
  533.9 10.0 fusion.220
  543.9 22.0 %add_add_fusion = f32[4096,1024]{1,0:T(8,128)} fusion(f32[4096,1024]{1,0:T(8,128)} %fusion.222, f32[4096,1024]{1,0:T(8,128)} %fusion.220, pred[]{:T(512)S(6)} %eq.107, bf16[64,1024]{1,0:T(8,128)(2,1)S(1)} %copy-done.70, f32[64,4096]{1,0:T(8,128)} %copy-done.58, f32[64,4096]{1,0:T(8,128)S(1)} %copy-done.57), kind=kOutput, calls=%fused_computation | convolution fusion | flops 579665920 | bytes 52559872 | tf_op jit(solution)/shard_map/dot_general | solution.py:26
  567.5 7.3 fusion.144
  575.8 2.2 multiply_reduce_fusion.6
  578.6 61.1 %all-reduce.13 = (f32[1024]{0:T(1024)S(1)}, f32[1024]{0:T(1024)S(1)}, f32[1024]{0:T(1024)S(1)}, f32[1024]{0:T(1024)S(1)}, f32[1024]{0:T(1024)S(1)}, /*index=5*/f32[4096]{0:T(1024)S(1)}, f32[1024]{0:T(1024)S(1)}) all-reduce(f32[1024]{0:T(1024)S(1)} %add_add_fusion.16, ...), channel_id=2, replica_groups=mesh['section'=2,'dp'=16] {'dp'}, use_global_device_ids=true, to_apply=%region_48.49.clone | all-reduce | flops 10240 | bytes 81920
  645.5 5.5 reduce-scatter.5.cloned.1.call-done
  651.0 183.1 %reduce-scatter.9.cloned.1.call-done = f32[64,4096]{1,0:T(8,128)} async-done(((f32[1024,4096]{1,0:T(8,128)}), f32[64,4096]{1,0:T(8,128)}) %reduce-scatter.9.cloned.1.call-update) | async-done | bytes 1048592 | tf_op jit(solution)/shard_map/reduce_scatter | solution.py:294
  834.2 182.9 %reduce-scatter.11.cloned.1.call-done = f32[256,1024]{1,0:T(8,128)} async-done(((f32[4096,1024]{1,0:T(8,128)}), f32[256,1024]{1,0:T(8,128)}) %reduce-scatter.11.cloned.1.call-update) | async-done | bytes 1048592 | tf_op jit(solution)/shard_map/reduce_scatter | solution.py:294
  (507 shorter events, 111.7 us)
Async XLA Ops:
  7.2 110.6 %copy-start.3 = (bf16[2,64,1024]{2,1,0:T(8,128)(2,1)S(1)}, bf16[2,64,1024]{2,1,0:T(8,128)(2,1)}, u32[]{:S(2)}) copy-start(bf16[2,64,1024]{2,1,0:T(8,128)(2,1)} %param.14) | copy-start | bytes 786436
  7.2 98.5 %all-gather.5.cloned.1.call-start = ((), (), s32[]{:S(2)}) async-start(), calls=%async_computation.4 | async-start | bytes 6684672 | tf_op jit(solution)/shard_map/all_gather | solution.py:231
  7.9 109.9 %all-gather.7.cloned.1.call-start = ((), (), s32[]{:S(2)}) async-start(), calls=%async_computation.5 | async-start | bytes 2228224 | tf_op jit(solution)/shard_map/all_gather | solution.py:232
  8.7 185.0 %all-gather.9.cloned.1.call-start = ((), (), s32[]{:S(2)}) async-start(), calls=%async_computation.6 | async-start | bytes 8912896 | tf_op jit(solution)/shard_map/all_gather | solution.py:236
  9.4 259.5 %all-gather.11.cloned.1.call-start = ((), (), s32[]{:S(2)}) async-start(), calls=%async_computation.7 | async-start | bytes 8912896 | tf_op jit(solution)/shard_map/all_gather | solution.py:238
  10.0 635.5 %reduce-scatter.7.cloned.1.call-start = ((), (), s32[]{:S(2)}) async-start(), calls=%async_computation.9 | async-start | bytes 4456448 | tf_op jit(solution)/shard_map/reduce_scatter | solution.py:294
  81.4 117.3 %copy-start.80 = (f32[1024]{0:T(1024)}, f32[1024]{0:T(1024)S(1)}, u32[]{:S(2)}) copy-start(f32[1024]{0:T(1024)S(1)} %add.502) | copy-start | bytes 12292
  81.4 187.5 %copy-start.122 = (f32[1024]{0:T(1024)}, f32[1024]{0:T(1024)S(1)}, u32[]{:S(2)}) copy-start(f32[1024]{0:T(1024)S(1)} %add.504) | copy-start | bytes 12292
  98.9 99.8 %copy-start.71 = (f32[1,4096]{1,0:T(1,128)}, f32[1,4096]{1,0:T(1,128)S(1)}, u32[]{:S(2)}) copy-start(f32[1,4096]{1,0:T(1,128)S(1)} %add.487) | copy-start | bytes 49156
  109.9 172.3 %copy-start.4 = (bf16[64,3072]{1,0:T(8,128)(2,1)}, bf16[64,3072]{1,0:T(8,128)(2,1)S(1)}, u32[]{:S(2)}) copy-start(bf16[64,3072]{1,0:T(8,128)(2,1)S(1)} %fusion.45) | copy-start | bytes 1179652
  110.9 82.8 %copy-start.72 = (f32[16,64]{1,0:T(8,128)}, f32[16,64]{1,0:T(8,128)S(1)}, u32[]{:S(2)}) copy-start(f32[16,64]{1,0:T(8,128)S(1)} %log_add_fusion.2) | copy-start | bytes 12292
  111.2 87.5 %copy-start.22 = (bf16[16,64,64]{2,1,0:T(8,128)(2,1)}, bf16[16,64,64]{2,1,0:T(8,128)(2,1)S(1)}, u32[]{:S(2)}) copy-start(bf16[16,64,64]{2,1,0:T(8,128)(2,1)S(1)} %convolution_convert_fusion.5) | copy-start | bytes 393220
  120.0 154.6 %copy-start.85 = (f32[64]{0:T(128)}, f32[64]{0:T(128)S(1)}, u32[]{:S(2)}) copy-start(f32[64]{0:T(128)S(1)} %broadcast_multiply_fusion.10) | copy-start | bytes 772
  120.2 154.4 %copy-start.89 = (f32[64]{0:T(128)}, f32[64]{0:T(128)S(1)}, u32[]{:S(2)}) copy-start(f32[64]{0:T(128)S(1)} %add_rsqrt_fusion.4) | copy-start | bytes 772
  198.7 70.2 %copy-start.51 = (f32[64,4096]{1,0:T(8,128)}, f32[64,4096]{1,0:T(8,128)S(1)}, u32[]{:S(2)}) copy-start(f32[64,4096]{1,0:T(8,128)S(1)} %fusion.36) | copy-start | bytes 3145732
  198.7 79.7 %copy-start.128 = (s32[64]{0:T(128)S(1)}, s32[64]{0:T(128)}, u32[]{:S(2)}) copy-start(s32[64]{0:T(128)} %get-tuple-element.126) | copy-start | bytes 772
  198.7 79.7 %copy-start.129 = (s32[64]{0:T(128)S(1)}, s32[64]{0:T(128)}, u32[]{:S(2)}) copy-start(s32[64]{0:T(128)} %get-tuple-element.122) | copy-start | bytes 772
  274.6 19.3 %copy-start.73 = (f32[16,64]{1,0:T(8,128)S(1)}, f32[16,64]{1,0:T(8,128)}, u32[]{:S(2)}) copy-start(f32[16,64]{1,0:T(8,128)} %copy-done.72) | copy-start | bytes 12292
  274.6 22.0 %copy-start = (bf16[1,1024,1024]{2,1,0:T(8,128)(2,1)S(1)}, bf16[1,1024,1024]{2,1,0:T(8,128)(2,1)}, u32[]{:S(2)}) copy-start(bf16[1,1024,1024]{2,1,0:T(8,128)(2,1)} %all-gather.7.cloned.1.call-done) | copy-start | bytes 6291460
  274.7 22.0 %copy-start.81 = (f32[1024]{0:T(1024)S(1)}, f32[1024]{0:T(1024)}, u32[]{:S(2)}) copy-start(f32[1024]{0:T(1024)} %copy-done.80) | copy-start | bytes 12292
  274.7 6.7 collective-permute-start
  303.4 13.8 %slice-start = ((s8[8388608]{0:T(1024)(128)(4,1)}), s8[4194304]{0:T(1024)(128)(4,1)S(1)}, s32[]{:S(2)}) async-start(s8[8388608]{0:T(1024)(128)(4,1)} %bitcast.372), calls=%async_computation.12 | async-start | bytes 8388608
  306.9 14.3 %collective-permute-start.1 = (bf16[64,1024]{1,0:T(8,128)(2,1)S(1)}, bf16[64,1024]{1,0:T(8,128)(2,1)S(1)}, u32[]{:S(2)}, u32[]{:S(2)}) collective-permute-start(bf16[64,1024]{1,0:T(8,128)(2,1)S(1)} %fusion.138), channel_id=1, source_target_pairs={{0,16},{1,17},{2,18},{3,19},{4,20},{5,21},{6,22},{7,23},{8,24},{9,... | collective-permute-start | bytes 393224 | tf_op jit(solution)/shard_map/ppermute | solution.py:12
  326.2 29.1 %slice-start.6 = ((s8[6291456]{0:T(1024)(128)(4,1)}), s8[2097152]{0:T(1024)(128)(4,1)S(1)}, s32[]{:S(2)}) async-start(s8[6291456]{0:T(1024)(128)(4,1)} %bitcast.378), calls=%async_computation.18 | async-start | bytes 4194304
  337.3 16.0 %copy-start.31 = (bf16[64,1024]{1,0:T(8,128)(2,1)}, bf16[64,1024]{1,0:T(8,128)(2,1)S(1)}, u32[]{:S(2)}) copy-start(bf16[64,1024]{1,0:T(8,128)(2,1)S(1)} %copy.158) | copy-start | bytes 393220
  348.7 16.6 %copy-start.23 = (bf16[16,64,64]{2,1,0:T(8,128)(2,1)S(1)}, bf16[16,64,64]{2,1,0:T(8,128)(2,1)}, u32[]{:S(2)}) copy-start(bf16[16,64,64]{2,1,0:T(8,128)(2,1)} %copy-done.22) | copy-start | bytes 393220
  353.3 16.4 %copy-start.6 = (f32[64,1024]{1,0:T(8,128)S(1)}, f32[64,1024]{1,0:T(8,128)}, u32[]{:S(2)}) copy-start(f32[64,1024]{1,0:T(8,128)} %copy-done.5) | copy-start | bytes 786436
  353.3 26.7 %collective-permute-start.2 = (bf16[64,1024]{1,0:T(8,128)(2,1)}, bf16[64,1024]{1,0:T(8,128)(2,1)}, u32[]{:S(2)}, u32[]{:S(2)}) collective-permute-start(bf16[64,1024]{1,0:T(8,128)(2,1)} %get-tuple-element.109), channel_id=1, source_target_pairs={{16,0},{17,1},{18,2},{19,3},{20,4},{21,5},{22,6},{23,7},{24,8},{25... | collective-permute-start | bytes 393224 | tf_op jit(solution)/shard_map/ppermute | solution.py:12
  359.7 14.6 %copy-start.18 = (bf16[64,1024]{0,1:T(8,128)(2,1)}, bf16[64,1024]{0,1:T(8,128)(2,1)S(1)}, u32[]{:S(2)}) copy-start(bf16[64,1024]{0,1:T(8,128)(2,1)S(1)} %copy.214) | copy-start | bytes 393220
  359.8 14.4 %copy-start.19 = (bf16[64,1024]{0,1:T(8,128)(2,1)}, bf16[64,1024]{0,1:T(8,128)(2,1)S(1)}, u32[]{:S(2)}) copy-start(bf16[64,1024]{0,1:T(8,128)(2,1)S(1)} %copy.213) | copy-start | bytes 393220
  399.1 18.9 %copy-start.15 = (f32[64,1024]{1,0:T(8,128)S(1)}, f32[64,1024]{1,0:T(8,128)}, u32[]{:S(2)}) copy-start(f32[64,1024]{1,0:T(8,128)} %copy-done.14) | copy-start | bytes 786436
  404.2 17.2 %copy-start.34 = (bf16[64,1024]{1,0:T(8,128)(2,1)}, bf16[64,1024]{1,0:T(8,128)(2,1)S(1)}, u32[]{:S(2)}) copy-start(bf16[64,1024]{1,0:T(8,128)(2,1)S(1)} %copy.173) | copy-start | bytes 393220
  407.2 14.2 %copy-start.36 = (bf16[64,1024]{1,0:T(8,128)(2,1)}, bf16[64,1024]{1,0:T(8,128)(2,1)S(1)}, u32[]{:S(2)}) copy-start(bf16[64,1024]{1,0:T(8,128)(2,1)S(1)} %reshape.851) | copy-start | bytes 393220
  410.9 15.1 %copy-start.56 = (f32[64,4096]{1,0:T(8,128)S(1)}, f32[64,4096]{1,0:T(8,128)}, u32[]{:S(2)}) copy-start(f32[64,4096]{1,0:T(8,128)} %copy-done.55) | copy-start | bytes 3145732
  410.9 15.1 %copy-start.59 = (f32[64,4096]{1,0:T(8,128)S(1)}, f32[64,4096]{1,0:T(8,128)}, u32[]{:S(2)}) copy-start(f32[64,4096]{1,0:T(8,128)} %copy-done.58) | copy-start | bytes 3145732
  419.1 6.9 collective-permute-start.3
  420.7 13.9 %slice-start.4 = ((s8[8388608]{0:T(1024)(128)(4,1)}), s8[4194304]{0:T(1024)(128)(4,1)S(1)}, s32[]{:S(2)}) async-start(s8[8388608]{0:T(1024)(128)(4,1)} %bitcast.376), calls=%async_computation.16 | async-start | bytes 8388608
  421.4 13.2 %slice-start.5 = ((s8[8388608]{0:T(1024)(128)(4,1)}), s8[4194304]{0:T(1024)(128)(4,1)S(1)}, s32[]{:S(2)}) async-start(s8[8388608]{0:T(1024)(128)(4,1)} %bitcast.376), calls=%async_computation.17 | async-start | bytes 8388608
  421.4 13.2 %copy-start.8 = (f32[64,1024]{1,0:T(8,128)S(1)}, f32[64,1024]{1,0:T(8,128)}, u32[]{:S(2)}) copy-start(f32[64,1024]{1,0:T(8,128)} %copy-done.7) | copy-start | bytes 786436
  421.4 13.2 %copy-start.120 = (f32[64]{0:T(128)S(1)}, f32[64]{0:T(128)}, u32[]{:S(2)}) copy-start(f32[64]{0:T(128)} %copy-done.119) | copy-start | bytes 772
  421.4 13.2 %copy-start.126 = (f32[64]{0:T(128)S(1)}, f32[64]{0:T(128)}, u32[]{:S(2)}) copy-start(f32[64]{0:T(128)} %fusion.311) | copy-start | bytes 772
  441.8 209.2 %reduce-scatter.5.cloned.1.call-start = ((), (), s32[]{:S(2)}) async-start(), calls=%async_computation.8 | async-start | bytes 13369344 | tf_op jit(solution)/shard_map/reduce_scatter | solution.py:294
  464.7 19.3 %copy-start.38 = (bf16[64,1024]{1,0:T(8,128)(2,1)}, bf16[64,1024]{1,0:T(8,128)(2,1)S(1)}, u32[]{:S(2)}) copy-start(bf16[64,1024]{1,0:T(8,128)(2,1)S(1)} %copy.188) | copy-start | bytes 393220
  469.3 14.7 %copy-start.41 = (bf16[64,1024]{1,0:T(8,128)(2,1)}, bf16[64,1024]{1,0:T(8,128)(2,1)S(1)}, u32[]{:S(2)}) copy-start(bf16[64,1024]{1,0:T(8,128)(2,1)S(1)} %reshape.859) | copy-start | bytes 393220
  484.1 350.1 %reduce-scatter.9.cloned.1.call-start = ((), (), s32[]{:S(2)}) async-start(), calls=%async_computation.10 | async-start | bytes 17825792 | tf_op jit(solution)/shard_map/reduce_scatter | solution.py:294
  520.3 13.6 %copy-start.50 = (bf16[64,1024]{1,0:T(8,128)(2,1)S(1)}, bf16[64,1024]{1,0:T(8,128)(2,1)}, u32[]{:S(2)}) copy-start(bf16[64,1024]{1,0:T(8,128)(2,1)} %copy-done.49) | copy-start | bytes 393220
  520.3 496.7 %reduce-scatter.11.cloned.1.call-start = ((), (), s32[]{:S(2)}) async-start(), calls=%async_computation.11 | async-start | bytes 17825792 | tf_op jit(solution)/shard_map/reduce_scatter | solution.py:294
  574.9 68.9 %copy-start.68 = (bf16[64,1024]{1,0:T(8,128)(2,1)S(1)}, bf16[64,1024]{1,0:T(8,128)(2,1)}, u32[]{:S(2)}) copy-start(bf16[64,1024]{1,0:T(8,128)(2,1)} %copy-done.67) | copy-start | bytes 393220
  (114 other events, 662.2 us)
Sparse Core Ops, SparseCore 0:
  10.3 65.1 all-gather.4
  77.7 40.0 all-gather.6
  120.0 73.6 all-gather.8
  195.7 73.1 all-gather.10
  441.9 69.6 reduce-scatter.6
  516.7 134.3 reduce-scatter.4
  656.3 177.8 reduce-scatter.8
  839.4 177.5 reduce-scatter.10
where the time goes:
time: 1030 us; the launch traced here: 1020 us
  waiting for transfers between devices  532 us (52%)
  matrix products  236 us (23%)
  blocking collectives  143 us (14%)
  local copies, waits for them, and re-layouts  49.4 us (5%)
  other arithmetic  31.6 us (3%)
  between operations  18.9 us (2%)
  starting transfers between devices  13.2 us (1%)
    reduce_scatter x4, waiting for transfers between devices, local(): summed = lax.psum_scatter(totals, 'dp', scatter_dimension=0, tiled=True)  372 us
    unnamed x2, blocking collectives  125 us
    dot_general x12, matrix products, inner_rows(): lax.dot_general(left, right, (((0,), (0,)), ((), ())), preferred_element_...  114 us
    all_gather x1, waiting for transfers between devices, local(): lax.all_gather(shards[7], 'dp', axis=1, tiled=True)  73.4 us
    all_gather x1, waiting for transfers between devices, local(): lax.all_gather(shards[9], 'dp', axis=1, tiled=True)  70.1 us
    dot_general x12, matrix products, times_transpose(): lax.dot_general(left, right, (((1,), (1,)), ((), ())), preferred_element_...  46.9 us
  transfers between devices with their start and end apart: 12, of which 8 were waited for; matrix products, arithmetic and copies ran while one was open for 19% of the time, Pallas kernels for 0%

commit v1 on v0

--- a/solution.py
+++ b/solution.py
@@ -1,6 +1,8 @@
 import jax
 import jax.numpy as jnp
 from jax import lax
+from jax.experimental import pallas as pl
+from jax.experimental.pallas import tpu as pltpu
 from jax.sharding import PartitionSpec as P
 
 HEAD = 64
@@ -296,6 +298,168 @@
     return (layer_outputs[None], input_grads[None]) + outputs
 
 
+MESH=pl.DeviceIdType.MESH
+
+def place():
+    s=lax.axis_index("section"); p=lax.axis_index("dp")
+    z=p//4; y=(p//2)%2; c=p%2
+    return s,z,y,c
+
+def gather_kernel(n,chunks,ahead,sibling, *refs):
+    own=refs[:n]; full=refs[n:2*n]; ssem,rsem,lsem=refs[2*n:]
+    K=len(chunks)
+    s,z,y,c=place()
+    inner=jnp.logical_or(z==1,z==2)
+    zo=jnp.where(z==1,0,3); zn=3-z; zon=3-zo
+    zi=jnp.where(z==0,1,2)
+    idx=lambda z,y,c:(z*2+y)*2+c
+    me=idx(z,y,c)
+    def rows(k,b):
+        j,r0,nr,_=chunks[k]
+        r=own[j].shape[0]
+        return full[j].at[pl.ds(pl.multiple_of(b*r+r0,nr),nr)]
+    def mine(k):
+        j,r0,nr,_=chunks[k]
+        return own[j].at[pl.ds(r0,nr)]
+    counts=[0]*K
+    def send(k,b,to,first=False):
+        i=counts[k]; counts[k]+=1
+        cp=pltpu.make_async_remote_copy(mine(k) if first else rows(k,b), rows(k,b), ssem.at[k,i], rsem.at[k,b], device_id=(s,to), device_id_type=MESH)
+        cp.start(); return cp
+    def recv(k,b):
+        pltpu.make_async_remote_copy(rows(k,b), rows(k,b), ssem.at[k,0], rsem.at[k,b], device_id=(s,me), device_id_type=MESH).wait_recv()
+    yo=1-y; co=1-c
+    sib=idx(z,y,co); ypart=idx(z,yo,c); other=idx(zn,y,c)
+    def late(k,take):
+        by_z=chunks[k][3]
+        take(k,idx(zon,y,c),*((sib,) if by_z else (ypart,sib)))
+        take(k,idx(zn,yo,c),sib)
+        take(k,idx(zon,yo,c),sib)
+    @pl.when(inner)
+    def _():
+        out=[]
+        loc=[]
+        def begin(k):
+            out.append(send(k,me,ypart,True))
+            out.append(send(k,me,other,True))
+            if sibling: out.append(send(k,me,sib,True))
+            l=pltpu.make_async_copy(mine(k),rows(k,me),lsem.at[k]); l.start(); loc.append(l)
+        def take(k,b,*to):
+            recv(k,b)
+            for t in to:
+                if t is sib and not sibling: continue
+                out.append(send(k,b,t))
+        for k in range(min(ahead,K)): begin(k)
+        for k in range(K):
+            if k+ahead<K: begin(k+ahead)
+            by_z=chunks[k][3]
+            take(k,idx(zo,y,c),other,sib)
+            take(k,idx(z,yo,c),sib)
+            take(k,idx(zn,y,c),ypart,sib)
+            take(k,idx(zo,yo,c),*((other,sib) if by_z else (sib,)))
+            if k>0: late(k-1,take)
+        late(K-1,take)
+        for k in range(K):
+            loc[k].wait()
+            if sibling:
+                for zz in range(4):
+                    for yy in range(2):
+                        recv(k,idx(zz,yy,co))
+        for o in out: o.wait_send()
+    counts[:]=[0]*K
+    @pl.when(jnp.logical_not(inner))
+    def _():
+        out=[]
+        def begin(k):
+            out.append(send(k,me,idx(zi,y,c),True))
+            out.append(send(k,me,idx(z,yo,c),True))
+        for k in range(min(ahead,K)): begin(k)
+        for k in range(K):
+            if k+ahead<K: begin(k+ahead)
+            recv(k,idx(z,yo,c))
+            out.append(send(k,idx(z,yo,c),idx(zi,y,c)))
+        for o in out: o.wait_send()
+
+def gather(shards, chunks, ahead, sibling, dp, mem=pl.ANY):
+    n=len(shards)
+    K=len(chunks)
+    return pl.pallas_call(
+        lambda *r: gather_kernel(n,chunks,ahead,sibling,*r),
+        out_shape=tuple(jax.ShapeDtypeStruct((dp*a.shape[0],)+a.shape[1:],a.dtype) for a in shards),
+        in_specs=[pl.BlockSpec(memory_space=mem)]*n,
+        out_specs=tuple([pl.BlockSpec(memory_space=mem)]*n),
+        scratch_shapes=[pltpu.SemaphoreType.DMA((K,16)),pltpu.SemaphoreType.DMA((K,16)),pltpu.SemaphoreType.DMA((K,))],
+        compiler_params=pltpu.CompilerParams(has_side_effects=True,vmem_limit_bytes=(60<<20) if mem!=pl.ANY else None),
+        name="gather_weights",
+    )(*shards)
+
+
+CHUNKS = (
+    (4, 0, 16, False),
+    (0, 0, 32, False), (0, 32, 32, True),
+    (1, 0, 64, False),
+    (2, 0, 32, False), (2, 32, 32, True),
+    (3, 0, 128, False), (3, 128, 128, True),
+)
+
+
+def middle(
+    block_input, crop_ids, out_grad, norm1_gain, norm1_shift, w_qkv, w_out, b_out,
+    norm2_gain, norm2_shift, w_up, b_up, w_down, b_down,
+):
+    dp = lax.axis_size("dp")
+    is_first = lax.axis_index("section") == 0
+    section, z, y, core = place()
+    inner = jnp.logical_or(z == 1, z == 2)
+    narrow = jnp.concatenate(
+        [norm1_gain[0], norm1_shift[0], b_out[0], norm2_gain[0], norm2_shift[0], b_down[0], b_up[0]]
+    ).reshape(5, 128)
+    narrow = jnp.concatenate([narrow, jnp.zeros((11, 128), jnp.bfloat16)])
+    w_qkv, w_out, w_up, w_down, narrow = gather(
+        (w_qkv[0], w_out[0], w_up[0], w_down[0], narrow), CHUNKS, 3, True, dp
+    )
+    narrow = narrow.reshape(dp, 16, 128)[:, :5].reshape(dp, 640)
+    small = [narrow[:, 64 * i : 64 * i + 64].reshape(-1) for i in range(6)]
+    gain_one, shift_one, b_out, gain_two, shift_two, b_down = small
+    b_up = narrow[:, 384:].reshape(-1)
+    weights = (
+        gain_one, shift_one, w_qkv, w_out, b_out, gain_two, shift_two, w_up, b_up, w_down, b_down,
+    )
+    pairs = [(i, i ^ 4) for i in range(dp)]
+    micro, rows, width = block_input.shape
+    joined = lambda own: jnp.concatenate([own, lax.ppermute(own, "dp", pairs)])
+    inputs = joined(block_input.reshape(-1, width))
+    cotangent = joined(out_grad.reshape(-1, width))
+    crops = joined(crop_ids.reshape(-1))
+    crops = crops + 1024 * (jnp.arange(crops.shape[0]) // rows)
+    saved = forward_layer(inputs.astype(jnp.float32), crops, weights)
+    passed = lax.ppermute(saved[-1].astype(jnp.bfloat16), "section", [(0, 1)])
+    source = jnp.where(is_first, inputs, passed)
+    later = forward_layer(source.astype(jnp.float32), crops, weights)
+    grad = cotangent.astype(jnp.float32)
+    grad_hidden, feed = backward_feed(grad, later, weights)
+    grad_in, attend = backward_attend(grad_hidden, later, crops, weights)
+    passed = lax.ppermute(grad_in.astype(jnp.bfloat16), "section", [(1, 0)])
+    grad = jnp.where(is_first, passed, cotangent).astype(jnp.float32)
+    grad_hidden, feed = backward_feed(grad, later, weights)
+    grad_in, attend = backward_attend(grad_hidden, later, crops, weights)
+    totals = attend + feed
+
+    def returned(values):
+        values = values.astype(jnp.bfloat16)
+        half = values.shape[0] // 2
+        back = lax.ppermute(values[half:], "dp", pairs)
+        return jnp.where(inner, values[:half], back).reshape(1, micro, rows, width)
+
+    summed = []
+    for item in totals:
+        item = jnp.where(inner, item, 0.0)
+        if item.ndim == 2:
+            item = item.astype(jnp.bfloat16)
+        summed.append(lax.psum_scatter(item, "dp", scatter_dimension=0, tiled=True).astype(jnp.float32)[None])
+    return (returned(later[-1]), returned(grad_in)) + tuple(summed)
+
+
 def solution(mesh):
     in_specs = (
         P(None, "dp", None),
@@ -328,4 +492,5 @@
         P("section", "dp", None),
         P("section", "dp"),
     )
-    return jax.shard_map(local, mesh=mesh, in_specs=in_specs, out_specs=out_specs, check_vma=False)
+    fits = mesh.shape["dp"] == 16 and mesh.shape["section"] == 2
+    return jax.shard_map(middle if fits else local, mesh=mesh, in_specs=in_specs, out_specs=out_specs, check_vma=False)

time: 1030 us -> 661 us (0.64)
  waiting for transfers between devices: 532 us -> 253 us
  matrix products: 236 us -> 138 us
  blocking collectives: 143 us -> 59.9 us
  Pallas kernels: 0 us -> 77.1 us
  starting transfers between devices: 13.2 us -> 51 us
  local copies, waits for them, and re-layouts: 49.4 us -> 27.4 us
    all_gather x4 -> x0, waiting for transfers between devices: 150 us -> none  [the longest x1 73.4 us: local(): lax.all_gather(shards[7], 'dp', axis=1, tiled=True)]
    reduce_scatter x4, waiting for transfers between devices: 372 us -> 234 us  [middle(): lax.psum_scatter(item, 'dp', scatter_dimension=0, tiled=True)]
    dot_general x12 -> x4, matrix products: 114 us -> 21.4 us  [inner_rows(): lax.dot_general(left, right, (((0,), (0,)), ((), ())), preferred_element_...]
    pallas_call x0 -> x1, Pallas kernels: none -> 77.1 us  [gather(): pl.pallas_call(lambda *r: gather_kernel(n, chunks, ahead, sibling, *r), o...]
    unnamed x2 -> x1, blocking collectives: 125 us -> 59.9 us
    ppermute x4 -> x7, starting transfers between devices: 12 us -> 50.3 us  [the longest x3 31.3 us: middle(): joined = lambda own: jnp.concatenate([own, lax.ppermute(own, 'dp', pairs)])]
    reshape x30 -> x0, local copies, waits for them, and re-layouts: 22.6 us -> none  [the longest x3 4.56 us: backward_attend(): grad_mixed = grad_mixed.reshape(queries.shape)]
    all_gather x1 -> x0, blocking collectives: 17.4 us -> none  [local(): lax.all_gather(shards[8], 'dp', axis=1, tiled=True)]
  transfers between devices with their start and end apart: 12 -> 11, of which waited for: 8 -> 5; matrix products, arithmetic and copies ran while one was open for 19% -> 14% of each run, Pallas kernels for 0% -> 12%
where the time goes in v1:
time: 661 us; the launch traced here: 650 us
  waiting for transfers between devices  253 us (38%)
  matrix products  138 us (21%)
  Pallas kernels  77.1 us (12%)
  blocking collectives  59.9 us (9%)
  starting transfers between devices  51 us (8%)
  local copies, waits for them, and re-layouts  27.4 us (4%)
  other arithmetic  27 us (4%)
  between operations  16.4 us (2%)
    reduce_scatter x4, waiting for transfers between devices, middle(): lax.psum_scatter(item, 'dp', scatter_dimension=0, tiled=True)  234 us
    pallas_call x1, Pallas kernels, gather(): pl.pallas_call(lambda *r: gather_kernel(n, chunks, ahead, sibling, *r), o...  77.1 us
    unnamed x1, blocking collectives  59.9 us
    dot_general x7, matrix products, times_transpose(): lax.dot_general(left, right, (((1,), (1,)), ((), ())), preferred_element_...  45.5 us
    ppermute x3, starting transfers between devices, middle(): joined = lambda own: jnp.concatenate([own, lax.ppermute(own, 'dp', pairs)])  31.3 us
    dot_general x2, matrix products, forward_layer(): jnp.dot(active, w_down, preferred_element_type=jnp.float32)  25.9 us
    dot_general x4, matrix products, inner_rows(): lax.dot_general(left, right, (((0,), (0,)), ((), ())), preferred_element_...  21.4 us
    dot_general x1, matrix products, forward_layer(): jnp.dot(squeezed, w_up, preferred_element_type=jnp.float32)  16.8 us
  transfers between devices with their start and end apart: 11, of which 5 were waited for; matrix products, arithmetic and copies ran while one was open for 14% of the time, Pallas kernels for 12%

profile of v1, /device:TPU:0, one launch (start us, length us, event | category | flops | bytes accessed | tf_op | source)
XLA Modules:
  0.0 649.9 jit_solution(10155085513863907848)
XLA Ops:
  7.2 3.1 collective-permute-start
  11.8 4.1 concatenate.34
  16.5 77.1 %gather_weights.1 = (bf16[1024,3072]{1,0:T(8,128)(2,1)}, bf16[1024,1024]{1,0:T(8,128)(2,1)}, bf16[1024,4096]{1,0:T(8,128)(2,1)}, bf16[4096,1024]{1,0:T(8,128)(2,1)}, bf16[256,128]{1,0:T(8,128)(2,1)}) custom-call(bf16[64,3072]{1,0:T(8,128)(2,1)} %bitcast.172, bf16[64,1024]{1,0:T(8,128)(2,1)} %bitcast.177, bf16[64,4096]{1,0:T(8,128)(2,1)} %bitcast.159, ...), custom_call_target="tpu_custom_call" | custom-call | tf_op jit(solution)/shard_map/gather_weights/pallas_call | solution.py:386
  96.1 1.2 fusion.99
  97.3 4.8 convolution_convert_fusion.1
  108.6 19.3 %fusion.89 = bf16[256,1024]{1,0:T(8,128)(2,1)S(1)} fusion(f32[256,1024]{1,0:T(8,128)} %copy-done.20, bf16[4096,1024]{1,0:T(8,128)(2,1)} %get-tuple-element.22, bf16[1024,4096]{1,0:T(8,128)(2,1)} %get-tuple-element.21, f32[4096]{0:T(1024)S(1)} %bitcast.180, f32[1024]{0:T(1024)S(1)} %reshape.404, f32[1024]{0:T(1024)S(1)} %reshape.402, ...), kind=kOutput, calls=%fused_computation.145 | convolution fusion | flops 4366270464 | bytes 18380800 | tf_op jit(solution)/shard_map/dot_general | solution.py:86
  128.0 3.9 collective-permute-start.2
  131.9 28.2 %collective-permute-start.4 = (bf16[128,1024]{1,0:T(8,128)(2,1)S(1)}, bf16[128,1024]{1,0:T(8,128)(2,1)}, u32[]{:S(2)}, u32[]{:S(2)}) collective-permute-start(bf16[128,1024]{1,0:T(8,128)(2,1)S(1)} %bitcast.154), channel_id=1, source_target_pairs={{0,4},{1,5},{2,6},{3,7},{4,0},{5,1},{6,2},{7,3},{8,12},{9,13},{10,... | collective-permute-start | bytes 786440 | tf_op jit(solution)/shard_map/ppermute | solution.py:430
  160.5 4.7 convolution_convert_fusion
  169.5 1.7 copy-done.9
  172.7 16.8 %multiply_convert_fusion.2 = (bf16[256,4096]{1,0:T(8,128)(2,1)}, f32[256,4096]{1,0:T(8,128)}, f32[256,4096]{1,0:T(8,128)}) fusion(f32[4096]{0:T(1024)S(1)} %bitcast.181, bf16[1024,4096]{1,0:T(8,128)(2,1)S(1)} %bitcast.191, f32[256,1024]{1,0:T(8,128)S(1)} %get-tuple-element.74, f32[256]{0:T(256)S(1)} %fusion.128, f32[256]{0:T(256)S(1)} %broadcast_multiply_fusion, ...), kind=kOutput, calls=%fused_computation.19 | convolution fusion | flops 2218000384 | bytes 19949568 | tf_op jit(solution)/shard_map/dot_general | solution.py:82
  189.5 12.8 %multiply_reduce_fusion.4 = (f32[256]{0:T(256)S(1)}, f32[256,1024]{1,0:T(8,128)}) fusion(f32[256,1024]{1,0:T(8,128)} %copy-done.3, f32[256]{0:T(256)S(1)} %broadcast_multiply_fusion, f32[1024]{0:T(1024)S(1)} %reshape.401, bf16[1024,4096]{1,0:T(8,128)(2,1)} %get-tuple-element.21, f32[256,4096]{1,0:T(8,128)} %get-tuple-element.52, ...), kind=kOutput, calls=%fused_computation.166 | convolution fusion | flops 4311744512 | bytes 27793408 | tf_op jit(solution)/shard_map/dot_general | solution.py:34
  202.3 1.9 fusion.175
  205.2 3.3 convolution_convert_fusion.5
  208.5 2.1 copy.75
  210.5 1.8 convolution_convert_fusion.4
  212.4 3.9 multiply_reduce_fusion.1
  216.3 1.2 multiply_convert_fusion.1
  218.8 2.0 fusion.104
  221.2 2.2 add_convert_fusion.6
  223.5 1.3 collective-permute-start.5
  224.8 14.7 %collective-permute-done.5 = bf16[256,1024]{1,0:T(8,128)(2,1)} collective-permute-done((bf16[256,1024]{1,0:T(8,128)(2,1)}, bf16[256,1024]{1,0:T(8,128)(2,1)}, u32[]{:S(2)}, u32[]{:S(2)}) %collective-permute-start.5) | collective-permute-done | bytes 524320 | tf_op jit(solution)/shard_map/ppermute | solution.py:442
  239.5 1.3 convert_reduce_fusion.3
  240.8 12.0 %convert_reduce_fusion = (f32[4096]{0:T(1024)S(1)}, bf16[256,4096]{1,0:T(8,128)(2,1)S(1)}) fusion(f32[256,4096]{1,0:T(8,128)} %get-tuple-element.52, f32[256,4096]{1,0:T(8,128)} %get-tuple-element.75, bf16[256,1024]{1,0:T(8,128)(2,1)S(1)} %get-tuple-element.38, bf16[4096,1024]{1,0:T(8,128)(2,1)} %get-tuple-element.22), kind=kOutput, calls=%fused_computation.11 | convolution fusion | flops 2164256768 | bytes 19415040 | tf_op jit(solution)/shard_map/dot_general | solution.py:34
  252.8 6.8 %multiply_reduce_fusion.2 = (f32[1024]{0:T(1024)S(1)}, f32[256]{0:T(256)S(1)}, f32[1024]{0:T(1024)S(1)}, f32[256,1024]{1,0:T(8,128)S(1)}) fusion(f32[256,1024]{1,0:T(8,128)S(1)} %copy-done.4, f32[256]{0:T(256)S(1)} %fusion.128, f32[256]{0:T(256)S(1)} %broadcast_multiply_fusion, f32[1024]{0:T(1024)S(1)} %reshape.401, ...), kind=kOutput, calls=%fused_computation.160 | convolution fusion | flops 2149578496 | bytes 12598272 | tf_op jit(solution)/shard_map/dot_general | solution.py:34
  262.1 2.0 select_convert_fusion.3
  264.5 3.3 convolution_convert_fusion.3
  267.8 2.1 copy.79
  269.9 1.8 convolution_convert_fusion.2
  271.7 4.0 multiply_reduce_fusion
  275.7 1.2 multiply_convert_fusion
  279.0 4.8 select_convert_fusion.2
  285.0 7.4 %select_convert_fusion.1 = bf16[1024,4096]{1,0:T(8,128)(2,1)} fusion(bf16[256,4096]{1,0:T(8,128)(2,1)} %copy-done.32, pred[]{:T(512)S(6)} %or.3, f32[256,1024]{1,0:T(8,128)S(1)} %copy-done.5, f32[256]{0:T(256)S(1)} %fusion.128, f32[256]{0:T(256)S(1)} %broadcast_multiply_fusion, f32[1024]{0:T(1024)S(1)} %reshape.402, f32[1024]{0:T(1024)S(1)} %reshape.401), kind=kOutput, calls=%fused_computation.1 | convolution fusion | flops 2157182976 | bytes 11544577 | tf_op jit(solution)/shard_map/dot_general | solution.py:28
  293.5 7.2 %select_convert_fusion = bf16[4096,1024]{1,0:T(8,128)(2,1)} fusion(bf16[256,4096]{1,0:T(8,128)(2,1)} %get-tuple-element.51, bf16[256,1024]{1,0:T(8,128)(2,1)S(1)} %copy-done.17, pred[]{:T(512)S(6)} %or.3), kind=kOutput, calls=%fused_computation | convolution fusion | flops 2155872256 | bytes 11010049 | tf_op jit(solution)/shard_map/dot_general | solution.py:28
  300.7 6.6 %fusion.83 = bf16[256,1024]{1,0:T(8,128)(2,1)S(1)} fusion(f32[256,1024]{1,0:T(8,128)S(1)} %copy-done.5, bf16[256,4096]{1,0:T(8,128)(2,1)} %get-tuple-element.51, bf16[4096,1024]{1,0:T(8,128)(2,1)} %get-tuple-element.22, f32[1024]{0:T(1024)S(1)} %reshape.404), kind=kOutput, calls=%fused_computation.134 | convolution fusion | flops 2148270080 | bytes 12062720 | tf_op jit(solution)/shard_map/dot_general | solution.py:86
  307.3 11.4 %collective-permute-start.3 = (bf16[128,1024]{1,0:T(8,128)(2,1)S(1)}, bf16[128,1024]{1,0:T(8,128)(2,1)S(1)}, u32[]{:S(2)}, u32[]{:S(2)}) collective-permute-start(bf16[128,1024]{1,0:T(8,128)(2,1)S(1)} %slice.97), channel_id=1, source_target_pairs={{0,4},{1,5},{2,6},{3,7},{4,0},{5,1},{6,2},{7,3},{8,12},{9,13},{10,... | collective-permute-start | bytes 786440 | tf_op jit(solution)/shard_map/ppermute | solution.py:451
  320.6 4.4 collective-permute-done.3
  325.7 5.4 fusion.172
  333.0 2.6 collective-permute-start.6
  335.6 59.9 %all-reduce.8 = (f32[1024]{0:T(1024)S(1)}, f32[1024]{0:T(1024)S(1)}, f32[1024]{0:T(1024)S(1)}, f32[1024]{0:T(1024)S(1)}, f32[1024]{0:T(1024)S(1)}, /*index=5*/f32[4096]{0:T(1024)S(1)}, f32[1024]{0:T(1024)S(1)}) all-reduce(f32[1024]{0:T(1024)S(1)} %get-tuple-element.89, ...), channel_id=2, replica_groups=mesh['section'=2,'dp'=16] {'dp'}, use_global_device_ids=true, to_apply=%region_23.24.clone | all-reduce | flops 10240 | bytes 81920
  399.6 1.7 slice_select_fusion
  401.3 1.6 bitcast_convert_fusion.3
  402.9 21.7 %reduce-scatter.5.cloned.1.call-done = bf16[64,3072]{1,0:T(8,128)(2,1)} async-done(((bf16[1024,3072]{1,0:T(8,128)(2,1)}), bf16[64,3072]{1,0:T(8,128)(2,1)}) %reduce-scatter.5.cloned.1.call-update) | async-done | bytes 393232 | tf_op jit(solution)/shard_map/reduce_scatter | solution.py:459
  424.6 1.9 bitcast_convert_fusion.2
  426.5 105.9 %reduce-scatter.9.cloned.1.call-done = bf16[64,4096]{1,0:T(8,128)(2,1)} async-done(((bf16[1024,4096]{1,0:T(8,128)(2,1)}), bf16[64,4096]{1,0:T(8,128)(2,1)}) %reduce-scatter.9.cloned.1.call-update) | async-done | bytes 524304 | tf_op jit(solution)/shard_map/reduce_scatter | solution.py:459
  532.4 2.1 bitcast_convert_fusion.1
  534.5 106.2 %reduce-scatter.11.cloned.1.call-done = bf16[256,1024]{1,0:T(8,128)(2,1)} async-done(((bf16[4096,1024]{1,0:T(8,128)(2,1)}), bf16[256,1024]{1,0:T(8,128)(2,1)}) %reduce-scatter.11.cloned.1.call-update) | async-done | bytes 524304 | tf_op jit(solution)/shard_map/reduce_scatter | solution.py:459
  640.7 2.1 bitcast_convert_fusion
  (171 shorter events, 34.1 us)
Async XLA Ops:
  7.2 394.1 %reduce-scatter.7.cloned.1.call-start = ((), (), s32[]{:S(2)}) async-start(), calls=%async_computation.5 | async-start | bytes 2228224 | tf_op jit(solution)/shard_map/reduce_scatter | solution.py:459
  7.2 87.8 %collective-permute-start = (bf16[128,1024]{1,0:T(8,128)(2,1)}, bf16[128,1024]{1,0:T(8,128)(2,1)S(1)}, u32[]{:S(2)}, u32[]{:S(2)}) collective-permute-start(bf16[128,1024]{1,0:T(8,128)(2,1)} %bitcast.144), channel_id=1, source_target_pairs={{0,4},{1,5},{2,6},{3,7},{4,0},{5,1},{6,2},{7,3},{8,12},{9,13},{10,... | collective-permute-start | bytes 786440 | tf_op jit(solution)/shard_map/ppermute | solution.py:430
  11.1 83.8 %collective-permute-start.1 = (s32[128]{0:T(128)S(1)}, s32[128]{0:T(128)S(1)}, u32[]{:S(2)}, u32[]{:S(2)}) collective-permute-start(s32[128]{0:T(128)S(1)} %concatenate.36), channel_id=1, source_target_pairs={{0,4},{1,5},{2,6},{3,7},{4,0},{5,1},{6,2},{7,3},{8,12},{9,13},{10,... | collective-permute-start | bytes 1544 | tf_op jit(solution)/shard_map/ppermute | solution.py:430
  103.7 1.8 copy-start.26
  104.5 2.0 copy-start.8
  104.5 2.0 copy-start.21
  107.4 1.0 copy-start.20
  108.6 23.2 %copy-start.25 = (bf16[2,64,1024]{2,1,0:T(8,128)(2,1)S(1)}, bf16[2,64,1024]{2,1,0:T(8,128)(2,1)}, u32[]{:S(2)}) copy-start(bf16[2,64,1024]{2,1,0:T(8,128)(2,1)} %param.16) | copy-start | bytes 786436
  128.0 32.0 %collective-permute-start.2 = (bf16[256,1024]{1,0:T(8,128)(2,1)S(1)}, bf16[256,1024]{1,0:T(8,128)(2,1)S(1)}, u32[]{:S(2)}, u32[]{:S(2)}) collective-permute-start(bf16[256,1024]{1,0:T(8,128)(2,1)S(1)} %fusion.89), channel_id=1, source_target_pairs={{0,16},{1,17},{2,18},{3,19},{4,20},{5,21},{6,22},{7,23},{8,24},{9,... | collective-permute-start | bytes 1572872 | tf_op jit(solution)/shard_map/ppermute | solution.py:436
  131.9 57.7 %collective-permute-start.4 = (bf16[128,1024]{1,0:T(8,128)(2,1)S(1)}, bf16[128,1024]{1,0:T(8,128)(2,1)}, u32[]{:S(2)}, u32[]{:S(2)}) collective-permute-start(bf16[128,1024]{1,0:T(8,128)(2,1)S(1)} %bitcast.154), channel_id=1, source_target_pairs={{0,4},{1,5},{2,6},{3,7},{4,0},{5,1},{6,2},{7,3},{8,12},{9,13},{10,... | collective-permute-start | bytes 786440 | tf_op jit(solution)/shard_map/ppermute | solution.py:430
  165.8 2.0 copy-start.10
  166.0 1.8 copy-start.13
  166.9 2.1 copy-start
  166.9 5.5 slice-start
  167.8 3.4 copy-start.9
  167.8 4.9 slice-start.1
  169.5 2.6 copy-start.22
  172.1 17.4 %copy-start.3 = (f32[256,1024]{1,0:T(8,128)}, f32[256,1024]{1,0:T(8,128)S(1)}, u32[]{:S(2)}) copy-start(f32[256,1024]{1,0:T(8,128)S(1)} %get-tuple-element.74) | copy-start | bytes 3145732
  204.2 1.0 copy-start.18
  212.3 3.9 copy-start.1
  212.3 6.4 slice-start.2
  216.3 1.2 copy-start.11
  216.3 2.0 copy-start.14
  216.3 2.5 slice-start.3
  218.8 2.4 copy-start.19
  223.5 16.0 %collective-permute-start.5 = (bf16[256,1024]{1,0:T(8,128)(2,1)}, bf16[256,1024]{1,0:T(8,128)(2,1)}, u32[]{:S(2)}, u32[]{:S(2)}) collective-permute-start(bf16[256,1024]{1,0:T(8,128)(2,1)} %add_convert_fusion.6), channel_id=1, source_target_pairs={{16,0},{17,1},{18,2},{19,3},{20,4},{21,5},{22,6},{23,7},{24,8},{25... | collective-permute-start | bytes 1572872 | tf_op jit(solution)/shard_map/ppermute | solution.py:442
  240.8 19.3 %copy-start.16 = (bf16[256,1024]{1,0:T(8,128)(2,1)}, bf16[256,1024]{1,0:T(8,128)(2,1)S(1)}, u32[]{:S(2)}) copy-start(bf16[256,1024]{1,0:T(8,128)(2,1)S(1)} %get-tuple-element.38) | copy-start | bytes 1572868
  240.8 12.0 %copy-start.4 = (f32[256,1024]{1,0:T(8,128)S(1)}, f32[256,1024]{1,0:T(8,128)}, u32[]{:S(2)}) copy-start(f32[256,1024]{1,0:T(8,128)} %copy-done.3) | copy-start | bytes 3145732
  252.8 6.8 %copy-start.32 = (bf16[256,4096]{1,0:T(8,128)(2,1)}, bf16[256,4096]{1,0:T(8,128)(2,1)S(1)}, u32[]{:S(2)}) copy-start(bf16[256,4096]{1,0:T(8,128)(2,1)S(1)} %get-tuple-element.40) | copy-start | bytes 6291460
  259.7 2.5 copy-start.23
  260.1 1.0 copy-start.6
  261.3 0.8 copy-start.30
  264.2 160.4 %reduce-scatter.5.cloned.1.call-start = ((), (), s32[]{:S(2)}) async-start(), calls=%async_computation.4 | async-start | bytes 6684672 | tf_op jit(solution)/shard_map/reduce_scatter | solution.py:459
  271.7 6.6 %copy-start.27 = (bf16[16,64,256]{2,1,0:T(8,128)(2,1)}, bf16[16,64,256]{2,1,0:T(8,128)(2,1)S(1)}, u32[]{:S(2)}) copy-start(bf16[16,64,256]{2,1,0:T(8,128)(2,1)S(1)} %convolution_convert_fusion.2) | copy-start | bytes 1572868
  271.7 4.0 copy-start.2
  275.7 1.2 copy-start.12
  275.7 2.0 copy-start.15
  277.7 0.8 copy-start.28
  278.2 0.8 copy-start.29
  283.8 1.3 copy-start.5
  283.8 248.6 %reduce-scatter.9.cloned.1.call-start = ((), (), s32[]{:S(2)}) async-start(), calls=%async_computation.6 | async-start | bytes 8912896 | tf_op jit(solution)/shard_map/reduce_scatter | solution.py:459
  292.4 1.0 copy-start.17
  292.4 348.3 %reduce-scatter.11.cloned.1.call-start = ((), (), s32[]{:S(2)}) async-start(), calls=%async_computation.7 | async-start | bytes 8912896 | tf_op jit(solution)/shard_map/reduce_scatter | solution.py:459
  300.7 18.0 %copy-start.31 = (u32[32]{0:T(128)S(1)}, u32[32]{0:T(128)}, u32[]{:S(2)}) copy-start(u32[32]{0:T(128)} %constant.156) | copy-start | bytes 388
  307.3 17.7 %collective-permute-start.3 = (bf16[128,1024]{1,0:T(8,128)(2,1)S(1)}, bf16[128,1024]{1,0:T(8,128)(2,1)S(1)}, u32[]{:S(2)}, u32[]{:S(2)}) collective-permute-start(bf16[128,1024]{1,0:T(8,128)(2,1)S(1)} %slice.97), channel_id=1, source_target_pairs={{0,4},{1,5},{2,6},{3,7},{4,0},{5,1},{6,2},{7,3},{8,12},{9,13},{10,... | collective-permute-start | bytes 786440 | tf_op jit(solution)/shard_map/ppermute | solution.py:451
  325.7 5.9 copy-start.7
  332.2 0.8 copy-start.24
  333.0 66.6 %collective-permute-start.6 = (bf16[128,1024]{1,0:T(8,128)(2,1)S(1)}, bf16[128,1024]{1,0:T(8,128)(2,1)S(1)}, u32[]{:S(2)}, u32[]{:S(2)}) collective-permute-start(bf16[128,1024]{1,0:T(8,128)(2,1)S(1)} %slice.99), channel_id=1, source_target_pairs={{0,4},{1,5},{2,6},{3,7},{4,0},{5,1},{6,2},{7,3},{8,12},{9,13},{10,... | collective-permute-start | bytes 786440 | tf_op jit(solution)/shard_map/ppermute | solution.py:451
Sparse Core Ops, SparseCore 0:
  264.3 70.9 reduce-scatter.6
  339.7 84.8 reduce-scatter.4
  428.7 103.7 reduce-scatter.8
  536.4 104.3 reduce-scatter.10

commit v2 on v0

--- a/solution.py
+++ b/solution.py
@@ -1,6 +1,10 @@
+import functools
+
 import jax
 import jax.numpy as jnp
 from jax import lax
+from jax.experimental import pallas as pl
+from jax.experimental.pallas import tpu as pltpu
 from jax.sharding import PartitionSpec as P
 
 HEAD = 64
@@ -296,6 +300,659 @@
     return (layer_outputs[None], input_grads[None]) + outputs
 
 
+MESH = pl.DeviceIdType.MESH
+F = jnp.float32
+B = jnp.bfloat16
+VECTORS = ("g1", "s1", "bo", "g2", "s2", "bd", "bu")
+PARTS = (
+    (4, 0, 16, False),
+    (0, 0, 32, False), (0, 32, 32, True),
+    (1, 0, 64, False),
+    (2, 0, 32, False), (2, 32, 32, True),
+    (3, 0, 128, False), (3, 128, 128, True),
+)
+AHEAD = 3
+SUMS = (
+    (3, 0, 128, False), (3, 128, 128, True),
+    (2, 0, 32, False), (2, 32, 32, True),
+    (1, 0, 64, False),
+    (0, 0, 32, False), (0, 32, 32, True),
+    (4, 0, 16, False),
+)
+A, O, C, G, DM, DU, DB, DQKV = range(8)
+
+
+def nt(left, right):
+    return lax.dot_general(left, right, (((1,), (1,)), ((), ())), preferred_element_type=F)
+
+
+def tn(left, right):
+    return lax.dot_general(left, right, (((0,), (0,)), ((), ())), preferred_element_type=F)
+
+
+def nn(left, right):
+    return jnp.dot(left, right, preferred_element_type=F)
+
+
+def tiles(total, step):
+    def run(body):
+        @pl.loop(0, total // step)
+        def _(i):
+            body(pl.ds(pl.multiple_of(i * step, step), step))
+
+    return run
+
+
+def normed(values):
+    centred = values - jnp.mean(values, axis=-1, keepdims=True)
+    scale = lax.rsqrt(jnp.mean(centred * centred, axis=-1, keepdims=True) + 1e-6)
+    return centred * scale, scale
+
+
+def norm_into(out, rows, gain, shift):
+    @tiles(rows.shape[0], 64)
+    def _(r):
+        hat, _ = normed(rows[r, :].astype(F))
+        out[r, :] = (hat * gain[...] + shift[...]).astype(B)
+
+
+def norm_back(rows, grad, base, out, gain, gain_sum, shift_sum):
+    gain_sum[...] = jnp.zeros_like(gain_sum)
+    shift_sum[...] = jnp.zeros_like(shift_sum)
+
+    @tiles(rows.shape[0], 64)
+    def _(r):
+        hat, scale = normed(rows[r, :].astype(F))
+        d = grad[r, :]
+        gain_sum[...] += jnp.sum(d * hat, axis=0, keepdims=True)
+        shift_sum[...] += jnp.sum(d, axis=0, keepdims=True)
+        d = d * gain[...]
+        mean = jnp.mean(d, axis=-1, keepdims=True)
+        along = jnp.mean(d * hat, axis=-1, keepdims=True)
+        out[r, :] = (base[r, :].astype(F) + scale * (d - mean - hat * along)).astype(out.dtype)
+
+
+def halves(pair):
+    low = lax.broadcasted_iota(jnp.int32, pair.shape, 1) < HEAD
+    zero = jnp.zeros_like(pair)
+    return jnp.where(low, pair, zero), jnp.where(low, zero, pair)
+
+
+def softmax(queries, keys, bias):
+    scores = nt(queries, keys) * HEAD**-0.5 + bias
+    raised = jnp.exp(scores - jnp.max(scores, axis=-1, keepdims=True))
+    return raised / jnp.sum(raised, axis=-1, keepdims=True)
+
+
+def attend(qkv, mixed, bias):
+    width = qkv.shape[1] // 3
+
+    @pl.loop(0, width // 128)
+    def _(i):
+        for t in range(qkv.shape[0] // 128):
+            r = pl.ds(t * 128, 128)
+            q, k, v = (qkv[r, pl.ds(pl.multiple_of(g * width + i * 128, 128), 128)] for g in range(3))
+            parts = [nn(softmax(a, k, bias[r, :]).astype(B), b) for a, b in zip(halves(q), halves(v))]
+            mixed[r, pl.ds(pl.multiple_of(i * 128, 128), 128)] = (parts[0] + parts[1]).astype(B)
+
+
+def attend_back(qkv, grad, bias):
+    width = qkv.shape[1] // 3
+
+    @pl.loop(0, width // 128)
+    def _(i):
+        for t in range(qkv.shape[0] // 128):
+            r = pl.ds(t * 128, 128)
+            cols = [pl.ds(pl.multiple_of(g * width + i * 128, 128), 128) for g in range(3)]
+            q, k, v = (qkv[r, c] for c in cols)
+            d = grad[r, cols[0]]
+            sums = None
+            for qh, kh, dh in zip(halves(q), halves(k), halves(d)):
+                p = softmax(qh, k, bias[r, :])
+                dp = nt(dh, v)
+                ds = (p * (dp - jnp.sum(dp * p, axis=-1, keepdims=True))).astype(B)
+                terms = (nn(ds, kh), tn(ds, qh), tn(p.astype(B), dh))
+                sums = terms if sums is None else [a + b for a, b in zip(sums, terms)]
+            qkv[r, cols[0]] = (sums[0] * HEAD**-0.5).astype(B)
+            qkv[r, cols[1]] = (sums[1] * HEAD**-0.5).astype(B)
+            qkv[r, cols[2]] = sums[2].astype(B)
+
+
+def relay(names, *refs):
+    ref = dict(zip(names, refs))
+    width = ref["x_own"].shape[1]
+    rows = ref["x_own"].shape[0]
+    ff = ref["w2"].shape[1]
+    shard = [ref[f"own{j}"] for j in range(5)]
+    full = [ref[f"w{j}"] for j in range(5)]
+    both = [ref[n] for n in ("a", "o", "c", "g", "dm", "du", "db", "dqkv")]
+    mine = [b.at[pl.ds(0, 2 * rows)] for b in both]
+    theirs = [b.at[pl.ds(2 * rows, 2 * rows)] for b in both]
+    vec = {n: ref["v_" + n] for n in VECTORS}
+    vsum = {n: ref["d_" + n] for n in VECTORS}
+    x, hidden, wide, dmixed, result = (ref[n] for n in ("x", "h", "wide", "do", "y"))
+    p = lax.axis_index("dp")
+    z, y, core = p // 4, (p // 2) % 2, p % 2
+    inner = jnp.logical_or(z == 1, z == 2)
+    section = lax.axis_index("section")
+    zo, zn = jnp.where(z == 1, 0, 3), 3 - z
+    zon = 3 - zo
+    zi = jnp.where(z == 0, 1, 2)
+
+    def idx(z, y, core):
+        return (z * 2 + y) * 2 + core
+
+    sibling, across, other = idx(z, y, 1 - core), idx(z, 1 - y, core), idx(zn, y, core)
+    outer_one, inner_one = idx(zo, y, core), idx(zi, y, core)
+
+    def remote(sec, src, dst, send_sem, recv_sem, to):
+        return pltpu.make_async_remote_copy(
+            src_ref=src, dst_ref=dst, send_sem=send_sem, recv_sem=recv_sem,
+            device_id=(sec, to), device_id_type=MESH,
+        )
+
+    class Flow:
+        def __init__(self, sec):
+            self.sec = sec
+            self.sent = []
+
+        def send(self, *args, sec=None):
+            copy = remote(self.sec if sec is None else sec, *args)
+            copy.start()
+            self.sent.append(copy)
+
+        def arrived(self, dst, recv_sem):
+            remote(self.sec, dst, dst, ref["idle_sem"].at[0], recv_sem, sibling).wait_recv()
+
+        def finish(self):
+            for copy in self.sent:
+                copy.wait_send()
+            self.sent = []
+
+    def piece(k, b):
+        j, first, count, _ = PARTS[k]
+        size = shard[j].shape[0]
+        return full[j].at[pl.ds(pl.multiple_of(b * size + first, count), count)]
+
+    def gather_steps(flow, is_inner):
+        used = [0] * len(PARTS)
+
+        def send(k, b, to, own=False):
+            j, first, count, _ = PARTS[k]
+            src = shard[j].at[pl.ds(first, count)] if own else piece(k, b)
+            flow.send(src, piece(k, b), ref["ag_send"].at[k, used[k]], ref["ag_recv"].at[k, b], to)
+            used[k] += 1
+
+        def take(k, b, *to):
+            flow.arrived(piece(k, b), ref["ag_recv"].at[k, b])
+            for target in to:
+                send(k, b, target)
+
+        def begin(k):
+            if is_inner:
+                for to in (across, other, sibling):
+                    send(k, p, to, own=True)
+                j, first, count, _ = PARTS[k]
+                pltpu.make_async_copy(shard[j].at[pl.ds(first, count)], piece(k, p), ref["ag_local"].at[k]).start()
+            else:
+                send(k, p, inner_one, own=True)
+                send(k, p, across, own=True)
+
+        def early(k):
+            if not is_inner:
+                take(k, across, inner_one)
+                return
+            by_z = PARTS[k][3]
+            take(k, idx(zo, y, core), other, sibling)
+            take(k, idx(z, 1 - y, core), sibling)
+            take(k, idx(zn, y, core), across, sibling)
+            take(k, idx(zo, 1 - y, core), *((other, sibling) if by_z else (sibling,)))
+
+        def late(k):
+            by_z = PARTS[k][3]
+            take(k, idx(zon, y, core), *((sibling,) if by_z else (across, sibling)))
+            take(k, idx(zn, 1 - y, core), sibling)
+            take(k, idx(zon, 1 - y, core), sibling)
+
+        def step(k):
+            if k == 0:
+                for first in range(AHEAD):
+                    begin(first)
+            if k + AHEAD < len(PARTS):
+                begin(k + AHEAD)
+            if k < len(PARTS):
+                early(k)
+            if is_inner and k > 0:
+                late(k - 1)
+
+        return step
+
+    def gathered(flow, j):
+        for k, part in enumerate(PARTS):
+            if part[0] == j:
+                j_, first, count, _ = part
+                pltpu.make_async_copy(shard[j].at[pl.ds(first, count)], piece(k, p), ref["ag_local"].at[k]).wait()
+                for b in range(8):
+                    block = 2 * b + 1 - core
+                    flow.arrived(piece(k, block), ref["ag_recv"].at[k, block])
+
+    def spread_vectors():
+        for i in range(8):
+            low = full[4][pl.ds(32 * i, 16), :].astype(F)
+            high = full[4][pl.ds(32 * i + 16, 16), :].astype(F)
+            joined = low + high
+            for n, name in enumerate(VECTORS[:6]):
+                vec[name][:, pl.ds(128 * i, 128)] = joined[n : n + 1]
+            for n, part in enumerate((low[6:7], low[7:8], high[6:7], high[7:8])):
+                vec["bu"][:, pl.ds(512 * i + 128 * n, 128)] = part
+
+    def exchange(flow, which):
+        flow.send(mine[which], theirs[which], ref["act_send"].at[which], ref["act_recv"].at[which], sibling)
+
+    def exchanged(flow, *which):
+        for w in which:
+            flow.arrived(theirs[w], ref["act_recv"].at[w])
+
+    def forward_attend(bias):
+        @tiles(3 * width, 1024)
+        def _(c):
+            mine[DQKV][:, c] = nn(mine[A][...], full[0][:, c]).astype(B)
+
+        attend(mine[DQKV], mine[O], bias)
+
+    def forward_out():
+        @tiles(width, 512)
+        def _(c):
+            hidden[:, c] = x[:, c].astype(F) + nn(mine[O][...], full[1][:, c]) + vec["bo"][:, c]
+
+        norm_into(mine[C], hidden, vec["g2"], vec["s2"])
+
+    def forward_up():
+        @tiles(ff, 1024)
+        def _(c):
+            u = nn(mine[C][...], full[2][:, c]) + vec["bu"][:, c]
+            phi = 0.5 + 0.5 * lax.erf(u * 0.5**0.5)
+            mine[G][:, c] = (u * phi).astype(B)
+            mine[DU][:, c] = (phi + u * (jnp.exp(-0.5 * u * u) * (0.5 / jnp.pi) ** 0.5)).astype(B)
+
+    def forward_down():
+        @tiles(width, 512)
+        def _(c):
+            result[:, c] = (hidden[:, c] + nn(mine[G][...], full[3][:, c]) + vec["bd"][:, c]).astype(B)
+
+    def backward_du():
+        vsum["bd"][...] = jnp.sum(mine[DM][...].astype(F), axis=0, keepdims=True)
+
+        @tiles(ff, 1024)
+        def _(c):
+            du = (nt(mine[DM][...], full[3][c, :]) * mine[DU][:, c].astype(F)).astype(B)
+            mine[DU][:, c] = du
+            vsum["bu"][:, c] = jnp.sum(du.astype(F), axis=0, keepdims=True)
+
+    def backward_dh():
+        @tiles(width, 512)
+        def _(c):
+            wide[:, c] = nt(mine[DU][...], full[2][c, :])
+
+        norm_back(hidden, wide, mine[DM], hidden, vec["g2"], vsum["g2"], vsum["s2"])
+        mine[DB][...] = hidden[...].astype(B)
+        vsum["bo"][...] = jnp.sum(mine[DB][...].astype(F), axis=0, keepdims=True)
+
+    def backward_attend(bias):
+        @tiles(width, 512)
+        def _(c):
+            dmixed[:, c] = nt(mine[DB][...], full[1][c, :]).astype(B)
+
+        attend_back(mine[DQKV], dmixed, bias)
+
+    def backward_da():
+        @tiles(width, 512)
+        def _(c):
+            wide[:, c] = nt(mine[DQKV][...], full[0][c, :])
+
+    def backward_dx():
+        norm_back(x, wide, hidden, x, vec["g1"], vsum["g1"], vsum["s1"])
+
+    def packed(which):
+        src, out = both[which], ref["packed"]
+        for i in range(width // 256):
+            first = src[:, pl.ds(256 * i, 128)].astype(F)
+            second = src[:, pl.ds(256 * i + 128, 128)].astype(F)
+            low = lax.broadcasted_iota(jnp.int32, first.shape, 1) < HEAD
+            even = jnp.where(low, first, pltpu.roll(second, HEAD, 1))
+            odd = jnp.where(low, pltpu.roll(first, HEAD, 1), second)
+            out[pl.ds(128 * i, 128), :] = jnp.where(core == 0, even, odd).T.astype(B)
+
+    def grad_down():
+        size = shard[3].shape[0]
+        for o in range(8):
+            c = pl.ds(pl.multiple_of(size * (2 * o + core), size), size)
+            full[3][pl.ds(size * o, size), :] = tn(both[G][:, c], both[DM][...]).astype(B)
+
+    def grad_of(j, left, right):
+        packed(left)
+
+        @tiles(both[right].shape[1], 512)
+        def _(c):
+            full[j][pl.ds(0, 8 * shard[j].shape[0]), c] = nn(ref["packed"][...], both[right][:, c]).astype(B)
+
+    def grad_vectors():
+        for o in range(8):
+            for n, name in enumerate(VECTORS[:6]):
+                ref["vp"][pl.ds(16 * o + n, 1), :] = vsum[name][:, pl.ds(128 * o, 128)]
+            for n in range(4):
+                ref["vp"][pl.ds(16 * o + 6 + n, 1), :] = vsum["bu"][:, pl.ds(512 * o + 128 * n, 128)]
+            ref["vp"][pl.ds(16 * o + 10, 6), :] = jnp.zeros((6, 128), F)
+
+    partial = [full[0], full[1], full[2], full[3], ref["vp"]]
+    sums = [ref[f"out{j}"] for j in range(4)] + [ref["vs"]]
+    NEAR, OWN, ALT, INNER, OUTER = range(5)
+    slots = [[ref[f"r{s}_{j}"] for j in range(5)] for s in range(5)]
+
+    def reducer(flow):
+        def slot(s, k):
+            j, first, count, _ = SUMS[k]
+            return slots[s][j].at[pl.ds(first, count)]
+
+        def part(k, zz, yy):
+            j, first, count, _ = SUMS[k]
+            size = partial[j].shape[0] // 8 if j == 4 else shard[j].shape[0]
+            return partial[j].at[pl.ds(pl.multiple_of((zz * 2 + yy) * size + first, count), count)]
+
+        def send(k, n, src, s, to):
+            flow.send(src, slot(s, k), ref["rs_send"].at[k, n], ref["rs_recv"].at[k, s], to)
+
+        def arrived(k, s):
+            flow.arrived(slot(s, k), ref["rs_recv"].at[k, s])
+
+        def add(k, dst, *more):
+            total = dst[...].astype(F)
+            for s in more:
+                total = total + slot(s, k)[...].astype(F)
+            return total
+
+        def issue(k):
+            by_z = SUMS[k][3]
+            send(k, 0, part(k, zn, 1 - y), NEAR, across)
+            if by_z:
+                send(k, 1, part(k, zon, 1 - y), ALT, other)
+                send(k, 4, part(k, zon, y), OUTER, other)
+            else:
+                send(k, 1, part(k, zon, 1 - y), ALT, across)
+                send(k, 6, part(k, zo, 1 - y), INNER, outer_one)
+            send(k, 2, part(k, z, 1 - y), OWN, across)
+
+        def middle(k):
+            by_z = SUMS[k][3]
+            dst = part(k, zn, y)
+            arrived(k, NEAR)
+            dst[...] = add(k, dst, NEAR).astype(dst.dtype)
+            send(k, 3, dst, INNER, other)
+            if not by_z:
+                dst = part(k, zon, y)
+                arrived(k, ALT)
+                dst[...] = add(k, dst, ALT).astype(dst.dtype)
+                send(k, 4, dst, OUTER, other)
+
+        def last(k):
+            by_z = SUMS[k][3]
+            dst = part(k, zo, y)
+            arrived(k, OUTER)
+            dst[...] = add(k, dst, OUTER).astype(dst.dtype)
+            send(k, 5, dst, OUTER, outer_one)
+            if by_z:
+                dst = part(k, zo, 1 - y)
+                arrived(k, ALT)
+                dst[...] = add(k, dst, ALT).astype(dst.dtype)
+                send(k, 6, dst, INNER, outer_one)
+            arrived(k, OWN)
+            arrived(k, INNER)
+            j, first, count, _ = SUMS[k]
+            sums[j][pl.ds(first, count), :] = add(k, part(k, z, y), OWN, INNER)
+
+        def pass_on(k):
+            arrived(k, INNER)
+            send(k, 0, slot(INNER, k), OWN, across)
+
+        def collect(k):
+            arrived(k, OUTER)
+            arrived(k, OWN)
+            j, first, count, _ = SUMS[k]
+            sums[j][pl.ds(first, count), :] = slot(OUTER, k)[...].astype(F) + slot(OWN, k)[...].astype(F)
+
+        def join_vectors():
+            flow.send(ref["vs"], ref["vt"], ref["vec_sem"].at[0], ref["vec_sem"].at[1], sibling)
+            flow.arrived(ref["vt"], ref["vec_sem"].at[1])
+            ref["out4"][...] = ref["vs"][...] + ref["vt"][...]
+
+        return issue, middle, last, pass_on, collect, join_vectors
+
+    def hand_out(flow, src, out, n):
+        flow.send(src.at[pl.ds(rows, rows)], out, ref["res_send"].at[n], ref["res_recv"].at[n], outer_one)
+        out[...] = src[pl.ds(0, rows), :]
+
+    def inner_program(sec):
+        flow = Flow(sec)
+        step = gather_steps(flow, True)
+        issue, middle, last, _, _, join_vectors = reducer(flow)
+        bias = ref["bias"]
+        half = pl.ds(0, rows)
+        own = [pltpu.make_async_copy(ref["bias_own"], bias.at[half], ref["tok_local"].at[0])]
+        if sec == 0:
+            own.append(pltpu.make_async_copy(ref["x_own"], x.at[half], ref["tok_local"].at[1]))
+        else:
+            own.append(pltpu.make_async_copy(ref["dy_own"], mine[DM].at[half], ref["tok_local"].at[1]))
+        for copy in own:
+            copy.start()
+
+        def tokens():
+            for copy in own:
+                copy.wait()
+            other_half = pl.ds(rows, rows)
+            flow.arrived(bias.at[other_half], ref["tok_recv"].at[0])
+            flow.arrived((x if sec == 0 else mine[DM]).at[other_half], ref["tok_recv"].at[1])
+
+        if sec == 0:
+            for k in range(2):
+                step(k)
+            gathered(flow, 4)
+            spread_vectors()
+            tokens()
+            norm_into(mine[A], x, vec["g1"], vec["s1"])
+            for k in range(2, 4):
+                step(k)
+            gathered(flow, 0)
+            forward_attend(bias)
+            for k in range(4, 5):
+                step(k)
+            gathered(flow, 1)
+            forward_out()
+            for k in range(5, 7):
+                step(k)
+            gathered(flow, 2)
+            forward_up()
+            for k in range(7, 9):
+                step(k)
+            gathered(flow, 3)
+            forward_down()
+            flow.send(result, x, ref["x_sem"].at[0], ref["x_sem"].at[1], p, sec=1)
+        else:
+            for k in range(9):
+                step(k)
+            for j in range(5):
+                gathered(flow, j)
+            spread_vectors()
+            tokens()
+            exchange(flow, DM)
+            flow.arrived(x, ref["x_sem"].at[1])
+            norm_into(mine[A], x, vec["g1"], vec["s1"])
+            forward_attend(bias)
+            forward_out()
+            forward_up()
+            forward_down()
+        hand_out(flow, result, ref["y_out"], 0)
+        for which in (A, O, C, G):
+            exchange(flow, which)
+        flow.finish()
+        if sec == 0:
+            flow.arrived(mine[DM], ref["x_sem"].at[3])
+            exchange(flow, DM)
+            backward_du()
+            exchange(flow, DU)
+            exchanged(flow, G, DM)
+            grad_down()
+            issue(0)
+            issue(1)
+            backward_dh()
+            exchange(flow, DB)
+            exchanged(flow, C, DU)
+            grad_of(2, C, DU)
+            issue(2)
+            issue(3)
+            backward_attend(bias)
+            exchange(flow, DQKV)
+            middle(0)
+            exchanged(flow, O, DB)
+            grad_of(1, O, DB)
+            issue(4)
+            backward_da()
+            exchanged(flow, A, DQKV)
+            grad_of(0, A, DQKV)
+            issue(5)
+            issue(6)
+            backward_dx()
+            grad_vectors()
+            issue(7)
+            hand_out(flow, x, ref["dx_out"], 1)
+            todo = [(1, 0), (2, 1), (3, 2), (4, 3), (5, 4), (6, 5), (7, 6)]
+        else:
+            backward_du()
+            exchange(flow, DU)
+            backward_dh()
+            exchange(flow, DB)
+            backward_attend(bias)
+            exchange(flow, DQKV)
+            backward_da()
+            backward_dx()
+            flow.send(x, mine[DM], ref["x_sem"].at[2], ref["x_sem"].at[3], p, sec=0)
+            exchanged(flow, G, DM)
+            grad_down()
+            issue(0)
+            issue(1)
+            exchanged(flow, C, DU)
+            grad_of(2, C, DU)
+            issue(2)
+            issue(3)
+            hand_out(flow, x, ref["dx_out"], 1)
+            exchanged(flow, O, DB)
+            grad_of(1, O, DB)
+            issue(4)
+            exchanged(flow, A, DQKV)
+            grad_of(0, A, DQKV)
+            issue(5)
+            issue(6)
+            grad_vectors()
+            issue(7)
+            middle(0)
+            todo = [(1, 0), (2, 1), (3, 2), (4, 3), (5, 4), (6, 5), (7, 6)]
+        for a, b in todo:
+            middle(a)
+            last(b)
+        last(7)
+        join_vectors()
+        flow.finish()
+
+    def outer_program(sec):
+        flow = Flow(sec)
+        step = gather_steps(flow, False)
+        _, _, _, pass_on, collect, join_vectors = reducer(flow)
+        half = pl.ds(rows, rows)
+        flow.send(ref["bias_own"], ref["bias"].at[half], ref["tok_send"].at[0], ref["tok_recv"].at[0], inner_one)
+        src, dst = (ref["x_own"], x) if sec == 0 else (ref["dy_own"], mine[DM])
+        flow.send(src, dst.at[half], ref["tok_send"].at[1], ref["tok_recv"].at[1], inner_one)
+        for k in range(len(PARTS)):
+            step(k)
+        for k in range(len(SUMS)):
+            pass_on(k)
+            if k:
+                collect(k - 1)
+        collect(len(SUMS) - 1)
+        join_vectors()
+        flow.arrived(ref["y_out"], ref["res_recv"].at[0])
+        flow.arrived(ref["dx_out"], ref["res_recv"].at[1])
+        flow.finish()
+
+    for sec in range(2):
+        pl.when(jnp.logical_and(inner, section == sec))(lambda sec=sec: inner_program(sec))
+        pl.when(jnp.logical_and(jnp.logical_not(inner), section == sec))(lambda sec=sec: outer_program(sec))
+
+
+def relay_call(x_own, dy_own, bias_own, shards, dp):
+    rows, width = x_own.shape
+    ff = shards[2].shape[1]
+    count = 2 * rows
+    inputs = {"x_own": x_own, "dy_own": dy_own, "bias_own": bias_own}
+    inputs.update({f"own{j}": item for j, item in enumerate(shards)})
+    outputs = {"y_out": ((rows, width), B), "dx_out": ((rows, width), B)}
+    outputs.update({f"out{j}": (item.shape, F) for j, item in enumerate(shards[:4])})
+    outputs["out4"] = ((16, 128), F)
+    scratch = {f"w{j}": ((dp * item.shape[0], item.shape[1]), B) for j, item in enumerate(shards)}
+    for name, cols in zip(("a", "o", "c", "g", "dm", "du", "db", "dqkv"), (1, 1, 1, 0, 1, 0, 1, 3)):
+        scratch[name] = ((2 * count, cols * width or ff), B)
+    scratch.update(x=((count, width), B), h=((count, width), F), wide=((count, width), F), do=((count, width), B))
+    scratch.update(y=((count, width), B), bias=((count, 128), F), packed=((width // 2, 2 * count), B))
+    for name in VECTORS:
+        scratch["v_" + name] = scratch["d_" + name] = ((1, ff if name == "bu" else width), F)
+    scratch.update(vp=((128, 128), F), vs=((16, 128), F), vt=((16, 128), F))
+    for s in range(5):
+        for j, item in enumerate(shards):
+            scratch[f"r{s}_{j}"] = (item.shape, F if j == 4 else B)
+    sems = dict(
+        ag_send=(len(PARTS), 16), ag_recv=(len(PARTS), dp), ag_local=(len(PARTS),), tok_local=(2,), tok_send=(2,),
+        tok_recv=(2,), x_sem=(4,), act_send=(8,), act_recv=(8,), res_send=(2,), res_recv=(2,),
+        rs_send=(len(SUMS), 7), rs_recv=(len(SUMS), 5), vec_sem=(2,), idle_sem=(1,),
+    )
+    names = [*inputs, *outputs, *scratch, *sems]
+    results = pl.pallas_call(
+        functools.partial(relay, names),
+        out_shape=[jax.ShapeDtypeStruct(*item) for item in outputs.values()],
+        in_specs=[pl.BlockSpec(memory_space=pl.ANY)] * len(inputs),
+        out_specs=[pl.BlockSpec(memory_space=pltpu.VMEM)] * len(outputs),
+        scratch_shapes=[pltpu.VMEM(*item) for item in scratch.values()]
+        + [pltpu.SemaphoreType.DMA(item) for item in sems.values()],
+        compiler_params=pltpu.CompilerParams(has_side_effects=True, vmem_limit_bytes=62 << 20),
+        name="relay",
+    )(*inputs.values())
+    return dict(zip(outputs, results))
+
+
+def middle(
+    block_input, crop_ids, out_grad, norm1_gain, norm1_shift, w_qkv, w_out, b_out,
+    norm2_gain, norm2_shift, w_up, b_up, w_down, b_down,
+):
+    core = lax.axis_index("dp") % 2
+    micro, rows, width = block_input.shape
+    crops = crop_ids + 1024 * jnp.arange(micro)[:, None]
+    crops = crops.reshape(-1)
+    bias = jnp.where(crops[:, None] == crops[None, :], 0.0, -1e30).astype(F)
+    narrow = jnp.concatenate([norm1_gain, norm1_shift, b_out, norm2_gain, norm2_shift, b_down])
+    empty = jnp.zeros_like(narrow)
+    narrow = jnp.where(core == 0, jnp.concatenate([narrow, empty], 1), jnp.concatenate([empty, narrow], 1))
+    narrow = jnp.concatenate([narrow, b_up.reshape(2, 128), jnp.zeros((8, 128), B)])
+    got = relay_call(
+        block_input.reshape(-1, width), out_grad.reshape(-1, width), bias,
+        (w_qkv[0], w_out[0], w_up[0], w_down[0], narrow), lax.axis_size("dp"),
+    )
+    sums = got["out4"]
+    narrow = jnp.where(core == 0, sums[:6, :64], sums[:6, 64:])[:, None]
+    grad_b_up = jnp.where(core == 0, sums[6:8], sums[8:10]).reshape(1, -1)
+    shape = (1, micro, rows, width)
+    return (
+        got["y_out"].reshape(shape), got["dx_out"].reshape(shape), narrow[0], narrow[1], got["out0"][None],
+        got["out1"][None], narrow[2], narrow[3], narrow[4], got["out2"][None], grad_b_up, got["out3"][None], narrow[5],
+    )
+
+
 def solution(mesh):
     in_specs = (
         P(None, "dp", None),
@@ -328,4 +985,5 @@
         P("section", "dp", None),
         P("section", "dp"),
     )
-    return jax.shard_map(local, mesh=mesh, in_specs=in_specs, out_specs=out_specs, check_vma=False)
+    fits = mesh.shape["dp"] == 16 and mesh.shape["section"] == 2
+    return jax.shard_map(middle if fits else local, mesh=mesh, in_specs=in_specs, out_specs=out_specs, check_vma=False)

time: 1030 us -> 332 us (0.32)
  waiting for transfers between devices: 532 us -> 0 us
  Pallas kernels: 0 us -> 317 us
  matrix products: 236 us -> 0 us
  blocking collectives: 143 us -> 0 us
  local copies, waits for them, and re-layouts: 49.4 us -> 10.4 us
  other arithmetic: 31.6 us -> 3.7 us
  between operations: 18.9 us -> 0.7 us
  starting transfers between devices: 13.2 us -> 0 us
    reduce_scatter x4 -> x0, waiting for transfers between devices: 372 us -> none  [local(): summed = lax.psum_scatter(totals, 'dp', scatter_dimension=0, tiled=True)]
    pallas_call x0 -> x1, Pallas kernels: none -> 317 us  [relay_call(): pl.pallas_call(functools.partial(relay, names), out_shape=[jax.ShapeDtype...]
    dot_general x57 -> x0, matrix products: 236 us -> none  [the longest x12 114 us: inner_rows(): lax.dot_general(left, right, (((0,), (0,)), ((), ())), preferred_element_...]
    all_gather x4 -> x0, waiting for transfers between devices: 150 us -> none  [the longest x1 73.4 us: local(): lax.all_gather(shards[7], 'dp', axis=1, tiled=True)]
    unnamed x2 -> x0, blocking collectives: 125 us -> none
    reshape x30 -> x0, local copies, waits for them, and re-layouts: 22.6 us -> none  [the longest x3 4.56 us: backward_attend(): grad_mixed = grad_mixed.reshape(queries.shape)]
    all_gather x1 -> x0, blocking collectives: 17.4 us -> none  [local(): lax.all_gather(shards[8], 'dp', axis=1, tiled=True)]
    reduce_sum x27 -> x0, other arithmetic: 13.3 us -> none  [the longest x11 4.47 us: norm_rows(): centred = values - jnp.mean(values, axis=-1, keepdims=True)]
  transfers between devices with their start and end apart: 12 -> 0, of which waited for: 8 -> 0; matrix products, arithmetic and copies ran while one was open for 19% -> 0% of each run, Pallas kernels for 0% -> 0%
where the time goes in v2:
time: 332 us
  Pallas kernels  317 us (95%)
  local copies, waits for them, and re-layouts  10.4 us (3%)
  other arithmetic  3.7 us (1%)
    pallas_call x1, Pallas kernels, relay_call(): pl.pallas_call(functools.partial(relay, names), out_shape=[jax.ShapeDtype...  317 us
    unnamed x30, local copies, waits for them, and re-layouts  9.66 us

profile of v2, /device:TPU:0, one launch (start us, length us, event | category | flops | bytes accessed | tf_op | source)
XLA Modules:
  0.0 331.5 jit_solution(12926991782485257084)
XLA Ops:
  0.7 0.0 copy-start.4
  0.7 0.7 copy-done.4
  1.4 0.1 pad.4.clone
  1.4 0.0 copy-start.5
  1.4 0.7 copy-done.5
  2.1 0.0 copy-start.9
  2.1 0.0 copy-start.10
  2.1 0.0 copy-start.11
  2.1 0.1 broadcast_add_fusion
  2.2 0.0 copy-start.6
  2.2 0.0 copy-start.7
  2.2 0.0 copy-start.8
  2.2 0.1 eq.22
  2.3 0.5 copy-done.9
  2.8 0.0 copy-done.10
  2.8 0.0 copy-done.11
  2.8 0.0 copy-done.6
  2.9 0.0 copy-done.7
  2.9 0.0 copy-done.8
  2.9 0.1 pad_select_fusion
  3.0 0.7 maximum_maximum_fusion.refs_7_
  3.7 0.7 compare_select_fusion.refs_2_
  4.4 316.7 %relay.1 = (bf16[128,1024]{1,0:T(8,128)(2,1)}, bf16[128,1024]{1,0:T(8,128)(2,1)}, f32[64,3072]{1,0:T(8,128)}, f32[64,1024]{1,0:T(8,128)}, f32[64,4096]{1,0:T(8,1...) custom-call(bf16[128,1024]{1,0:T(8,128)(2,1)} %bitcast.20, bf16[128,1024]{1,0:T(8,128)(2,1)} %bitcast.21, ...), custom_call_target="tpu_custom_call" | custom-call | tf_op jit(solution)/shard_map/relay/pallas_call | solution.py:916
  321.1 0.0 copy-start.2
  321.1 1.3 slice_select_fusion.1
  322.4 0.8 slice_select_fusion
  323.3 0.5 fusion
  323.8 1.7 copy.33
  325.5 1.7 copy.34
  327.1 0.0 copy-done.2
  327.1 0.0 copy-start.3
  327.2 0.0 copy-start.1
  327.2 0.9 copy.35
  328.0 0.2 copy-done.3
  328.2 0.7 copy.36
  328.9 0.0 copy-done.1
  328.9 0.0 copy-start
  328.9 1.0 copy.37
  329.9 0.6 copy-done
  330.6 1.0 copy.38
  (4 shorter events, 0.1 us)
Async XLA Ops:
  0.7 0.7 copy-start.4
  1.4 0.7 copy-start.5
  2.1 0.7 copy-start.9
  2.1 0.7 copy-start.10
  2.1 0.7 copy-start.11
  2.2 0.7 copy-start.6
  2.2 0.7 copy-start.7
  2.2 0.7 copy-start.8
  321.1 6.0 %copy-start.2 = (f32[64,3072]{1,0:T(8,128)S(1)}, f32[64,3072]{1,0:T(8,128)}, u32[]{:S(2)}) copy-start(f32[64,3072]{1,0:T(8,128)} %get-tuple-element.23) | copy-start | bytes 2359300
  327.1 1.1 copy-start.3
  327.2 1.8 copy-start.1
  328.9 1.6 copy-start
